TPU v7x, 256 devices: a whole 4x4x8 slice. The times are simulated.
256 devices in a mesh: tm: 32 (over x, z_hi, core), rows: 8 (over y, z_lo).
Axes of the slice: x: 4, y: 4, z: 8 (z_hi: 4, z_lo: 2; z = z_hi * 2 + z_lo), core: 2. Of those that a mesh axis runs over, the one named last changes fastest.
Arguments:
- latents: bfloat16 [32, 64, 104, 384], P('tm', 'rows'), may hold values from -6 to 6
- norm_gain: float32 [384], replicated, may hold values from 0.1 to 1.9
- conv_weight: bfloat16 [3, 3, 3, 384, 384], replicated, may hold values from -0.0625 to 0.0625
- up_weight: bfloat16 [3, 384, 768], replicated, may hold values from -0.1875 to 0.1875
Outputs:
- upsampled: bfloat16 [64, 64, 104, 384], P('tm', 'rows')
All inputs are finite; a program needn't handle non-finite values.
Results may differ from a plain program's by a relative error of at most 0.0052.
Values may be sent and summed in bfloat16 or wider, within the bound.
No kernel may reach another device: no remote copies, remote signals or barrier semaphores. Data moves between devices by JAX's collectives and lax.ppermute only.
A program may use at most 64 MiB of HBM per device.

v0:
```python
import jax
import jax.numpy as jnp
from jax import lax
from jax.sharding import PartitionSpec as P

EPS = 1e-06


def shifted(block, axis, distance):
    devices = range(lax.axis_size(axis))
    route = [(i - distance, i) for i in devices if i - distance in devices]
    return lax.ppermute(block, axis, route)


def extended(cells, sides, width):
    for axis, dim in sides:
        count = lax.axis_size(axis)
        ends = count - 1
        head = lax.slice_in_dim(cells, 0, width, axis=dim)
        tail = lax.slice_in_dim(cells, cells.shape[dim] - width, cells.shape[dim], axis=dim)
        cells = jnp.concatenate(
            [
                lax.ppermute(tail, axis, [(i, (i + 1) % count) for i in range(ends)]),
                cells,
                lax.ppermute(head, axis, [((i + 1) % count, i) for i in range(ends)]),
            ],
            axis=dim,
        )
    return cells


def convolve(inputs, kernel, padding):
    return lax.conv_general_dilated(
        inputs,
        kernel,
        (1, 1, 1),
        padding,
        dimension_numbers=("NDHWC", "DHWIO", "NDHWC"),
        preferred_element_type=jnp.float32,
    )


def back_frames(source):
    previous = shifted(source, "tm", 1)
    second = shifted(source, "tm", 2)
    return (second, previous)


def local(latents, norm_gain, conv_weight, up_weight):
    values = latents.astype(jnp.float32)
    scaled = values * lax.rsqrt(jnp.mean(values * values, axis=-1, keepdims=True) + EPS) * norm_gain
    activated = jax.nn.silu(scaled).astype(jnp.bfloat16)
    earlier, recent = back_frames(activated)
    window = extended(jnp.concatenate([earlier, recent, activated], 0), (("rows", 1),), 1)
    convolved = convolve(window[None], conv_weight, ((0, 0), (0, 0), (1, 1)))[0]
    block_out = (values + convolved).astype(jnp.bfloat16)
    older_out, recent_out = back_frames(block_out)
    stacked = jnp.concatenate([older_out, recent_out, block_out], 0)
    doubled = convolve(stacked[None], up_weight[:, None, None], ((0, 0), (0, 0), (0, 0)))[0][
        0
    ].astype(jnp.bfloat16)
    rows_here = latents.shape[1]
    columns = latents.shape[2]
    channels = latents.shape[3]
    return doubled.reshape(rows_here, columns, 2, channels).transpose(2, 0, 1, 3)


def solution(mesh):
    placed = (P("tm", "rows", None, None), P(), P(), P())
    return jax.shard_map(
        local, mesh=mesh, in_specs=placed, out_specs=P("tm", "rows", None, None), check_vma=False
    )
```

profile of v0, /device:TPU:3, one launch (start us, length us, event | category | flops | bytes accessed | tf_op | source)
XLA Modules:
  0.0 142.0 jit_solution(13127816989649803362)
XLA Ops:
  0.0 0.0 copy-start
  0.0 1.4 fusion.20
  1.4 0.1 copy.26
  1.5 0.1 copy.27
  1.6 1.5 %fusion.27 = bf16[1,8,104,384]{3,1,2,0:T(8,128)(2,1)S(1)} fusion(f32[384]{0:T(512)} %param.5, f32[8,104]{0,1:T(8,128)S(1)} %copy.27, bf16[1,8,104,384]{3,2,1,0:T(8,128)(2,1)} %param.4), kind=kLoop, calls=%fused_computation.26 | loop fusion | flops 2555904 | bytes 1282816 | tf_op jit(solution)/shard_map/convert_element_type | solution.py:52
  3.1 5.5 %collective-permute-start.1 = (bf16[1,8,104,384]{3,1,2,0:T(8,128)(2,1)S(1)}, bf16[1,8,104,384]{3,1,2,0:T(8,128)(2,1)S(1)}, u32[]{:S(2)}, u32[]{:S(2)}) collective-permute-start(bf16[1,8,104,384]{3,1,2,0:T(8,128)(2,1)S(1)} %fusion.27), channel_id=1, source_target_pairs={{0,8},{8,16},{16,24},{24,32},{32,40},{40,48},{48,56},{56,64},{64,7... | collective-permute-start | bytes 1916936 | tf_op jit(solution)/shard_map/ppermute | solution.py:12
  8.6 6.1 %collective-permute-start = (bf16[1,8,104,384]{3,1,2,0:T(8,128)(2,1)S(1)}, bf16[1,8,104,384]{3,1,2,0:T(8,128)(2,1)S(1)}, u32[]{:S(2)}, u32[]{:S(2)}) collective-permute-start(bf16[1,8,104,384]{3,1,2,0:T(8,128)(2,1)S(1)} %fusion.27), channel_id=1, source_target_pairs={{0,16},{8,24},{16,32},{24,40},{32,48},{40,56},{48,64},{56,72},{64,... | collective-permute-start | bytes 1916936 | tf_op jit(solution)/shard_map/ppermute | solution.py:12
  14.7 9.4 %collective-permute-done.1 = bf16[1,8,104,384]{3,1,2,0:T(8,128)(2,1)S(1)} collective-permute-done((bf16[1,8,104,384]{3,1,2,0:T(8,128)(2,1)S(1)}, bf16[1,8,104,384]{3,1,2,0:T(8,128)(2,1)S(1)}, u32[]{:S(2)}, u32[]{:S(2)}) %collective-permute-start.1) | collective-permute-done | bytes 639008 | tf_op jit(solution)/shard_map/ppermute | solution.py:12
  24.1 15.6 %collective-permute-done = bf16[1,8,104,384]{3,1,2,0:T(8,128)(2,1)S(1)} collective-permute-done((bf16[1,8,104,384]{3,1,2,0:T(8,128)(2,1)S(1)}, bf16[1,8,104,384]{3,1,2,0:T(8,128)(2,1)S(1)}, u32[]{:S(2)}, u32[]{:S(2)}) %collective-permute-start) | collective-permute-done | bytes 639008 | tf_op jit(solution)/shard_map/ppermute | solution.py:12
  39.7 0.8 pad_maximum_fusion.3
  40.6 16.1 %collective-permute-start.2 = (bf16[3,1,104,384]{3,1,2,0:T(2,128)(2,1)S(1)}, bf16[3,1,104,384]{3,1,2,0:T(2,128)(2,1)S(1)}, u32[]{:S(2)}, u32[]{:S(2)}) collective-permute-start(bf16[3,1,104,384]{3,1,2,0:T(2,128)(2,1)S(1)} %get-tuple-element.5), channel_id=1, source_target_pairs={{0,1},{1,2},{2,3},{3,4},{4,5},{5,6},{6,7},{8,9},{9,10},{10,11},{11... | collective-permute-start | bytes 718856 | tf_op jit(solution)/shard_map/ppermute | solution.py:23
  56.7 1.3 collective-permute-start.3
  58.0 4.3 %collective-permute-done.2 = bf16[3,1,104,384]{3,1,2,0:T(2,128)(2,1)S(1)} collective-permute-done((bf16[3,1,104,384]{3,1,2,0:T(2,128)(2,1)S(1)}, bf16[3,1,104,384]{3,1,2,0:T(2,128)(2,1)S(1)}, u32[]{:S(2)}, u32[]{:S(2)}) %collective-permute-start.2) | collective-permute-done | bytes 239648 | tf_op jit(solution)/shard_map/ppermute | solution.py:23
  62.3 10.4 %collective-permute-done.3 = bf16[3,1,104,384]{3,1,2,0:T(2,128)(2,1)S(1)} collective-permute-done((bf16[3,1,104,384]{3,1,2,0:T(2,128)(2,1)S(1)}, bf16[3,1,104,384]{3,1,2,0:T(2,128)(2,1)S(1)}, u32[]{:S(2)}, u32[]{:S(2)}) %collective-permute-start.3) | collective-permute-done | bytes 239648 | tf_op jit(solution)/shard_map/ppermute | solution.py:25
  72.6 0.0 slice-start
  72.7 3.1 %maximum_bitcast_fusion = bf16[3,10,1,104,384]{4,1,3,0,2:T(8,128)(2,1)S(1)} fusion(bf16[3,1,104,384]{3,1,2,0:T(2,128)(2,1)S(1)} %collective-permute-done.3, bf16[1,8,104,384]{3,1,2,0:T(8,128)(2,1)S(1)} %fusion.27, bf16[1,8,104,384]{3,1,2,0:T(8,128)(2,1)S(1)} %collective-permute-done.1, bf16[1,8,104,384]{3,1,2,0:T(8,128)(2,1)S(1)} %collective-permute-done, ...), kind=kLoop, calls=%fused_computation.2 | loop fusion | flops 11980800 | bytes 4792320 | tf_op jit(solution)/shard_map/broadcast_in_dim | solution.py:55
  75.8 0.0 slice-start.1
  75.8 0.5 pad
  76.3 0.0 copy-start.2
  76.4 0.9 copy.30
  77.3 0.1 slice.11
  77.4 0.0 slice-done
  77.4 0.5 slice-done.1
  77.9 0.0 copy-done.2
  77.9 9.8 %fusion.17 = f32[1,8,8,14,384]{4,2,3,1,0:T(8,128)S(1)} fusion(bf16[3,3,3,384,384]{4,3,2,1,0:T(8,128)(2,1)S(1)} %bitcast.32, bf16[3,10,1,7,2,384]{5,3,4,1,0,2:T(8,128)(2,1)S(1)} %slice.11, bf16[3,10,1,8,14,384]{5,3,4,1,0,2:T(8,128)(2,1)S(1)} %copy.30, pred[8,14]{0,1:T(8,128)(4,1)S(1)} %copy-done.2), kind=kOutput, calls=%fused_computation.18 | convolution fusion | flops 7143702528 | bytes 12242032 | tf_op jit(solution)/shard_map/conv_general_dilated | solution.py:33
  87.7 0.0 copy-start.1
  87.7 0.7 copy.31
  88.4 0.4 copy-done.1
  88.8 0.1 fusion.28
  88.9 1.9 %collective-permute-start.5 = (bf16[1,8,104,384]{3,1,2,0:T(8,128)(2,1)S(1)}, bf16[1,8,104,384]{3,1,2,0:T(8,128)(2,1)S(1)}, u32[]{:S(2)}, u32[]{:S(2)}) collective-permute-start(bf16[1,8,104,384]{3,1,2,0:T(8,128)(2,1)S(1)} %fusion.28), channel_id=1, source_target_pairs={{0,8},{8,16},{16,24},{24,32},{32,40},{40,48},{48,56},{56,64},{64,7... | collective-permute-start | bytes 1916936 | tf_op jit(solution)/shard_map/ppermute | solution.py:12
  90.9 2.5 %collective-permute-start.4 = (bf16[1,8,104,384]{3,1,2,0:T(8,128)(2,1)S(1)}, bf16[1,8,104,384]{3,1,2,0:T(8,128)(2,1)S(1)}, u32[]{:S(2)}, u32[]{:S(2)}) collective-permute-start(bf16[1,8,104,384]{3,1,2,0:T(8,128)(2,1)S(1)} %fusion.28), channel_id=1, source_target_pairs={{0,16},{8,24},{16,32},{24,40},{32,48},{40,56},{48,64},{56,72},{64,... | collective-permute-start | bytes 1916936 | tf_op jit(solution)/shard_map/ppermute | solution.py:12
  93.3 8.3 %collective-permute-done.5 = bf16[1,8,104,384]{3,1,2,0:T(8,128)(2,1)S(1)} collective-permute-done((bf16[1,8,104,384]{3,1,2,0:T(8,128)(2,1)S(1)}, bf16[1,8,104,384]{3,1,2,0:T(8,128)(2,1)S(1)}, u32[]{:S(2)}, u32[]{:S(2)}) %collective-permute-start.5) | collective-permute-done | bytes 639008 | tf_op jit(solution)/shard_map/ppermute | solution.py:12
  101.6 34.2 %collective-permute-done.4 = bf16[1,8,104,384]{3,1,2,0:T(8,128)(2,1)S(1)} collective-permute-done((bf16[1,8,104,384]{3,1,2,0:T(8,128)(2,1)S(1)}, bf16[1,8,104,384]{3,1,2,0:T(8,128)(2,1)S(1)}, u32[]{:S(2)}, u32[]{:S(2)}) %collective-permute-start.4) | collective-permute-done | bytes 639008 | tf_op jit(solution)/shard_map/ppermute | solution.py:12
  135.8 0.3 pad_maximum_fusion
  136.1 0.0 copy-done
  136.1 1.8 %fusion.11 = bf16[1,8,8,13,768]{4,2,3,1,0:T(8,128)(2,1)S(1)} fusion(bf16[3,384,768]{2,1,0:T(8,128)(2,1)S(1)} %copy-done, bf16[3,8,8,13,384]{4,1,3,2,0:T(8,128)(2,1)S(1)} %bitcast.30), kind=kOutput, calls=%fused_computation.16 | convolution fusion | flops 1472839680 | bytes 4964352 | tf_op jit(solution)/shard_map/conv_general_dilated | solution.py:33
  137.9 0.2 copy.34
  138.1 1.2 convert_element_type.20
  139.4 2.6 %copy.35 = bf16[2,8,104,384]{3,2,1,0:T(8,128)(2,1)} copy(bf16[2,8,104,384]{3,0,1,2:T(2,128)(2,1)} %bitcast.29) | data formatting | bytes 2555904 | tf_op jit(solution)/shard_map/transpose | solution.py:65
  (2 shorter events, 0.0 us)
Async XLA Ops:
  0.0 136.1 %copy-start = (bf16[3,384,768]{2,1,0:T(8,128)(2,1)S(1)}, bf16[3,384,768]{2,1,0:T(8,128)(2,1)}, u32[]{:S(2)}) copy-start(bf16[3,384,768]{2,1,0:T(8,128)(2,1)} %param.7) | copy-start | bytes 5308420
  3.1 21.0 %collective-permute-start.1 = (bf16[1,8,104,384]{3,1,2,0:T(8,128)(2,1)S(1)}, bf16[1,8,104,384]{3,1,2,0:T(8,128)(2,1)S(1)}, u32[]{:S(2)}, u32[]{:S(2)}) collective-permute-start(bf16[1,8,104,384]{3,1,2,0:T(8,128)(2,1)S(1)} %fusion.27), channel_id=1, source_target_pairs={{0,8},{8,16},{16,24},{24,32},{32,40},{40,48},{48,56},{56,64},{64,7... | collective-permute-start | bytes 1916936 | tf_op jit(solution)/shard_map/ppermute | solution.py:12
  8.6 31.1 %collective-permute-start = (bf16[1,8,104,384]{3,1,2,0:T(8,128)(2,1)S(1)}, bf16[1,8,104,384]{3,1,2,0:T(8,128)(2,1)S(1)}, u32[]{:S(2)}, u32[]{:S(2)}) collective-permute-start(bf16[1,8,104,384]{3,1,2,0:T(8,128)(2,1)S(1)} %fusion.27), channel_id=1, source_target_pairs={{0,16},{8,24},{16,32},{24,40},{32,48},{40,56},{48,64},{56,72},{64,... | collective-permute-start | bytes 1916936 | tf_op jit(solution)/shard_map/ppermute | solution.py:12
  40.6 21.7 %collective-permute-start.2 = (bf16[3,1,104,384]{3,1,2,0:T(2,128)(2,1)S(1)}, bf16[3,1,104,384]{3,1,2,0:T(2,128)(2,1)S(1)}, u32[]{:S(2)}, u32[]{:S(2)}) collective-permute-start(bf16[3,1,104,384]{3,1,2,0:T(2,128)(2,1)S(1)} %get-tuple-element.5), channel_id=1, source_target_pairs={{0,1},{1,2},{2,3},{3,4},{4,5},{5,6},{6,7},{8,9},{9,10},{10,11},{11... | collective-permute-start | bytes 718856 | tf_op jit(solution)/shard_map/ppermute | solution.py:23
  56.7 16.0 %collective-permute-start.3 = (bf16[3,1,104,384]{3,1,2,0:T(2,128)(2,1)S(1)}, bf16[3,1,104,384]{3,1,2,0:T(2,128)(2,1)S(1)}, u32[]{:S(2)}, u32[]{:S(2)}) collective-permute-start(bf16[3,1,104,384]{3,1,2,0:T(2,128)(2,1)S(1)} %get-tuple-element.6), channel_id=1, source_target_pairs={{1,0},{2,1},{3,2},{4,3},{5,4},{6,5},{7,6},{9,8},{10,9},{11,10},{12... | collective-permute-start | bytes 718856 | tf_op jit(solution)/shard_map/ppermute | solution.py:25
  72.6 4.8 %slice-start = ((s8[7962624]{0:T(1024)(128)(4,1)}), s8[4194304]{0:T(1024)(128)(4,1)S(1)}, s32[]{:S(2)}) async-start(s8[7962624]{0:T(1024)(128)(4,1)} %bitcast.31), calls=%async_computation | async-start | bytes 8388608
  75.8 2.1 %slice-start.1 = ((s8[7962624]{0:T(1024)(128)(4,1)}), s8[3768320]{0:T(1024)(128)(4,1)S(1)}, s32[]{:S(2)}) async-start(s8[7962624]{0:T(1024)(128)(4,1)} %bitcast.31), calls=%async_computation.1 | async-start | bytes 7536640
  76.3 1.5 %copy-start.2 = (pred[8,14]{0,1:T(8,128)(4,1)S(1)}, pred[8,14]{0,1:T(8,128)(4,1)}, u32[]{:S(2)}) copy-start(pred[8,14]{0,1:T(8,128)(4,1)} %constant.19) | copy-start | bytes 340
  87.7 1.1 copy-start.1
  88.9 12.7 %collective-permute-start.5 = (bf16[1,8,104,384]{3,1,2,0:T(8,128)(2,1)S(1)}, bf16[1,8,104,384]{3,1,2,0:T(8,128)(2,1)S(1)}, u32[]{:S(2)}, u32[]{:S(2)}) collective-permute-start(bf16[1,8,104,384]{3,1,2,0:T(8,128)(2,1)S(1)} %fusion.28), channel_id=1, source_target_pairs={{0,8},{8,16},{16,24},{24,32},{32,40},{40,48},{48,56},{56,64},{64,7... | collective-permute-start | bytes 1916936 | tf_op jit(solution)/shard_map/ppermute | solution.py:12
  90.9 44.9 %collective-permute-start.4 = (bf16[1,8,104,384]{3,1,2,0:T(8,128)(2,1)S(1)}, bf16[1,8,104,384]{3,1,2,0:T(8,128)(2,1)S(1)}, u32[]{:S(2)}, u32[]{:S(2)}) collective-permute-start(bf16[1,8,104,384]{3,1,2,0:T(8,128)(2,1)S(1)} %fusion.28), channel_id=1, source_target_pairs={{0,16},{8,24},{16,32},{24,40},{32,48},{40,56},{48,64},{56,72},{64,... | collective-permute-start | bytes 1916936 | tf_op jit(solution)/shard_map/ppermute | solution.py:12
where the time goes:
time: 142 us
  waiting for transfers between devices  82.1 us (58%)
  starting transfers between devices  33.4 us (24%)
  matrix products  11.7 us (8%)
  local copies, waits for them, and re-layouts  7.37 us (5%)
  other arithmetic  7.29 us (5%)
    ppermute x4, waiting for transfers between devices, shifted(): return lax.ppermute(block, axis, route)  67.5 us
    ppermute x1, starting transfers between devices, extended(): lax.ppermute(tail, axis, [(i, (i + 1) % count) for i in range(ends)])  16.1 us
    ppermute x4, starting transfers between devices, shifted(): return lax.ppermute(block, axis, route)  16 us
    conv_general_dilated x2, matrix products, convolve(): lax.conv_general_dilated(inputs, kernel, (1, 1, 1), padding, dimension_nu...  11.7 us
    ppermute x1, waiting for transfers between devices, extended(): lax.ppermute(head, axis, [((i + 1) % count, i) for i in range(ends)])  10.4 us
    ppermute x1, waiting for transfers between devices, extended(): lax.ppermute(tail, axis, [(i, (i + 1) % count) for i in range(ends)])  4.3 us
    broadcast_in_dim x1, other arithmetic, local(): convolved = convolve(window[None], conv_weight, ((0, 0), (0, 0), (1, 1)))[0]  3.12 us
  transfers between devices with their start and end apart: 6, of which 6 were waited for; matrix products, arithmetic and copies ran while one was open for 0% of the time, Pallas kernels for 0%

commit v1 on v0

v1 whole, which is shorter than its diff:
```python
import functools

import jax
import jax.numpy as jnp
from jax import lax
from jax.experimental import pallas as pl
from jax.experimental.pallas import tpu as pltpu
from jax.sharding import PartitionSpec as P

EPS = 1e-06
AXES = ("tm", "rows")
PAIRS = 16
BLOCKS = 8
PITCH = 112
CUT = 72


def device(pair, core, block):
    return (pair * 2 + core) * BLOCKS + block


def routes():
    every = [(m, c, r) for m in range(PAIRS) for c in range(2) for r in range(BLOCKS)]
    swap = [(device(m, c, r), device(m, 1 - c, r)) for m, c, r in every]
    ahead = [(device(m, c, r), device(m + 1, c, r)) for m, c, r in every if m + 1 < PAIRS]

    def back(m):
        return m // 4 * 4 + (m - 1) % 4

    behind = [(device(m, c, r), device(back(m), c, r)) for m, c, r in every if m + 2 < PAIRS]
    behind_again = [(device(back(m), c, r), device(m + 2, c, r)) for m, c, r in every if m + 2 < PAIRS]
    edges = []
    for m, c, r in every:
        to = r + (1 if c else -1)
        if 0 <= to < BLOCKS:
            edges.append((device(m, c, r), device(m, 1 - c, to)))
    return swap, ahead, behind, behind_again, edges


def send(block, route):
    return lax.ppermute(block, AXES, route)


def activate(values, gain):
    scaled = values * lax.rsqrt(jnp.mean(values * values, axis=-1, keepdims=True) + EPS) * gain
    return scaled / (1.0 + jnp.exp(-scaled))


def fill_taps(core, cells, outer, inner, gain, taps):
    rows, width, channels = cells.shape[1:]
    scale = gain[...]
    first = core == 0

    def frame(f, _):
        for q in range(rows + 2):
            if q == 0:
                values = jnp.where(first, outer[f, 0], inner[f, 0])
            elif q == rows + 1:
                values = jnp.where(first, inner[f, 0], outer[f, 0])
            else:
                values = cells[f, q - 1]
            active = activate(values.astype(jnp.float32), scale)
            active = jnp.concatenate([active, jnp.zeros((PITCH - width, channels), jnp.float32)], 0)
            columns = (pltpu.roll(active, 1, 0), active, pltpu.roll(active, PITCH - 1, 0))
            columns = [column.astype(jnp.bfloat16) for column in columns]
            for b in range(3):
                i = q - b
                if 0 <= i < rows:
                    for k in range(3):
                        start = (b * 3 + k) * channels
                        taps[f, i, :, start : start + channels] = columns[k]
        return 0

    lax.fori_loop(0, 2, frame, 0)


def product(taps, frames, weight):
    lhs = taps[frames]
    lhs = lhs.reshape(-1, lhs.shape[-1])
    return jnp.dot(lhs, weight, preferred_element_type=jnp.float32)


def late_terms(cells, taps, weight, total):
    rows, width, channels = cells.shape[1:]
    size = rows * PITCH
    both = product(taps, slice(0, 2), weight[2])
    total[...] = both.reshape(2, size, channels)
    for f in range(2):
        for i in range(rows):
            total[f, i * PITCH : i * PITCH + width] += cells[f, i].astype(jnp.float32)
    total[1] += product(taps, slice(0, 1), weight[1])


def early_terms(taps, weight):
    size = taps.shape[1] * PITCH
    both = product(taps, slice(0, 2), weight[0])
    more = product(taps, slice(1, 2), weight[1])
    return both[:size] + more, both[size:]


def stage_own(core, cells, outer, inner, gain, weight, total, taps):
    fill_taps(core[0], cells, outer, inner, gain, taps)
    late_terms(cells, taps, weight, total)


def stage_middle(core, cells, outer, inner, gain, weight, up, own, total, partial, taps):
    fill_taps(core[0], cells, outer, inner, gain, taps)
    terms = early_terms(taps, weight)
    first = (own[0] + terms[0]).astype(jnp.bfloat16)
    second = (own[1] + terms[1]).astype(jnp.bfloat16)
    dot = functools.partial(jnp.dot, preferred_element_type=jnp.float32)
    partial[0] = dot(first, up[2])
    partial[1] = dot(first, up[1]) + dot(second, up[2])
    late_terms(cells, taps, weight, total)


def stage_old(core, cells, outer, inner, gain, weight, up, own, partial, keep, give, taps):
    rows, width, channels = cells.shape[1:]
    fill_taps(core[0], cells, outer, inner, gain, taps)
    terms = early_terms(taps, weight)
    first = (own[0] + terms[0]).astype(jnp.bfloat16)
    second = (own[1] + terms[1]).astype(jnp.bfloat16)
    dot = functools.partial(jnp.dot, preferred_element_type=jnp.float32)
    even = partial[0] + dot(first, up[0]) + dot(second, up[1])
    odd = partial[1] + dot(second, up[0])

    def write(target, value):
        for k in range(2):
            for i in range(rows):
                piece = value[i * PITCH : i * PITCH + width, k * channels : (k + 1) * channels]
                target[k, i] = piece.astype(jnp.bfloat16)

    @pl.when(core[0] == 0)
    def _():
        write(keep, even)
        write(give, odd)

    @pl.when(core[0] != 0)
    def _():
        write(keep, odd)
        write(give, even)


def call(body, outs, flops, core, *args):
    rows, channels = args[0].shape[1], args[0].shape[3]
    whole = pl.BlockSpec(memory_space=pltpu.VMEM)
    return pl.pallas_call(
        body,
        out_shape=outs,
        in_specs=[pl.BlockSpec(memory_space=pltpu.SMEM)] + [whole] * len(args),
        out_specs=[whole] * len(outs),
        scratch_shapes=[pltpu.VMEM((2, rows, PITCH, 9 * channels), jnp.bfloat16)],
        compiler_params=pltpu.CompilerParams(vmem_limit_bytes=44 << 20),
        cost_estimate=pl.CostEstimate(flops=flops, bytes_accessed=10 << 20, transcendentals=0),
    )(core, *args)


def local(latents, norm_gain, conv_weight, up_weight):
    swap, ahead, behind, behind_again, edges = routes()
    core = lax.axis_index("tm") % 2
    rows, width, channels = latents.shape[1] // 2, latents.shape[2], latents.shape[3]
    gain = norm_gain.reshape(1, channels)
    weight = conv_weight.reshape(3, 9 * channels, channels)
    mark = core.reshape(1).astype(jnp.int32)
    size = rows * PITCH

    kept = lax.dynamic_slice_in_dim(latents, core * rows, rows, 1)
    given = lax.dynamic_slice_in_dim(latents, (1 - core) * rows, rows, 1)
    taken = send(given, swap)
    own = jnp.where(
        core == 0, jnp.concatenate([kept, taken], 0), jnp.concatenate([taken, kept], 0)
    )

    def borders(pair):
        outer = lax.dynamic_slice_in_dim(pair, core * (rows - 1), 1, 1)
        inner = lax.dynamic_slice_in_dim(pair, (1 - core) * (rows - 1), 1, 1)
        return send(outer, edges), send(inner, swap)

    middle = send(own, ahead)
    away = send(own[:, :, :CUT], behind)
    own_borders = borders(own)
    totals = jax.ShapeDtypeStruct((2, size, channels), jnp.float32)
    (own_total,) = call(stage_own, [totals], 10**10, mark, own, *own_borders, gain, weight)
    away = send(away, behind_again)
    near = send(middle[:, :, CUT:], ahead)
    middle_total, partial = call(
        stage_middle,
        [totals, jax.ShapeDtypeStruct((2, size, 2 * channels), jnp.float32)],
        2 * 10**10,
        mark,
        middle,
        *borders(middle),
        gain,
        weight,
        up_weight,
        own_total,
    )
    old = jnp.concatenate([away, near], 2)
    half = jax.ShapeDtypeStruct((2, rows, width, channels), jnp.bfloat16)
    keep, give = call(
        stage_old,
        [half, half],
        10**10,
        mark,
        old,
        *borders(old),
        gain,
        weight,
        up_weight,
        middle_total,
        partial,
    )
    got = send(give, swap)
    return jnp.where(
        core == 0, jnp.concatenate([keep, got], 1), jnp.concatenate([got, keep], 1)
    )


def solution(mesh):
    placed = (P("tm", "rows", None, None), P(), P(), P())
    return jax.shard_map(
        local, mesh=mesh, in_specs=placed, out_specs=P("tm", "rows", None, None), check_vma=False
    )
```

time: 142 us -> 103 us (0.73)
  the two profiles are of different devices: /device:TPU:3 before, /device:TPU:29 now
where the time goes in v1:
time: 103 us; the launch traced here: 102 us
  starting transfers between devices  42.2 us (41%)
  Pallas kernels  33.2 us (32%)
  waiting for transfers between devices  19.8 us (19%)
  local copies, waits for them, and re-layouts  4.68 us (5%)
  other arithmetic  1.45 us (1%)
    ppermute x12, starting transfers between devices, send(): return lax.ppermute(block, AXES, route)  42.2 us
    pallas_call x3, Pallas kernels, call(): pl.pallas_call(body, out_shape=outs, in_specs=[pl.BlockSpec(memory_space=...  33.2 us
    ppermute x12, waiting for transfers between devices, send(): return lax.ppermute(block, AXES, route)  19.8 us
    unnamed x7, local copies, waits for them, and re-layouts  3.31 us
  transfers between devices with their start and end apart: 12, of which 5 were waited for; matrix products, arithmetic and copies ran while one was open for 0% of the time, Pallas kernels for 22%

profile of v1, /device:TPU:29, one launch (start us, length us, event | category | flops | bytes accessed | tf_op | source)
XLA Modules:
  0.0 101.5 jit_solution(4533069047464146240)
XLA Ops:
  0.0 1.1 %constant_dynamic-slice_fusion.7 = (bf16[1,4,104,384]{3,2,1,0:T(8,128)(2,1)S(1)}, bf16[1,4,104,384]{3,2,1,0:T(8,128)(2,1)S(1)}) fusion(bf16[1,8,104,384]{3,2,1,0:T(8,128)(2,1)} %param.4, s32[]{:T(128)S(6)} %select_n.42, s32[]{:T(128)S(6)} %select_n.43), kind=kLoop, calls=%fused_computation.11 | loop fusion | bytes 1277960 | tf_op jit(solution)/shard_map/dynamic_slice | solution.py:167
  1.1 0.8 collective-permute-start
  1.9 1.2 %collective-permute-done = bf16[1,4,104,384]{3,2,1,0:T(8,128)(2,1)S(1)} collective-permute-done((bf16[1,4,104,384]{3,2,1,0:T(8,128)(2,1)S(1)}, bf16[1,4,104,384]{3,2,1,0:T(8,128)(2,1)S(1)}, u32[]{:S(2)}, u32[]{:S(2)}) %collective-permute-start) | collective-permute-done | bytes 319520 | tf_op jit(solution)/shard_map/ppermute | solution.py:41
  3.1 0.0 copy-start.2
  3.1 0.1 maximum_select_fusion.1.cells
  3.3 7.9 %collective-permute-start.1 = (bf16[2,4,72,384]{3,2,1,0:T(8,128)(2,1)S(1)}, bf16[2,4,72,384]{3,2,1,0:T(8,128)(2,1)S(1)}, u32[]{:S(2)}, u32[]{:S(2)}) collective-permute-start(bf16[2,4,72,384]{3,2,1,0:T(8,128)(2,1)S(1)} %slice.8), channel_id=1, source_target_pairs={{0,48},{1,49},{2,50},{3,51},{4,52},{5,53},{6,54},{7,55},{8,56},{9,... | collective-permute-start | bytes 1327112 | tf_op jit(solution)/shard_map/ppermute | solution.py:41
  11.3 0.7 collective-permute-start.10
  12.1 2.5 %collective-permute-start.9 = (bf16[2,1,104,384]{3,2,1,0:T(8,128)(2,1)S(1)}, bf16[2,1,104,384]{3,2,1,0:T(8,128)(2,1)S(1)}, u32[]{:S(2)}, u32[]{:S(2)}) collective-permute-start(bf16[2,1,104,384]{3,2,1,0:T(8,128)(2,1)S(1)} %get-tuple-element.14), channel_id=1, source_target_pairs={{1,8},{2,9},{3,10},{4,11},{5,12},{6,13},{7,14},{8,1},{9,2},{10,3},... | collective-permute-start | bytes 479240 | tf_op jit(solution)/shard_map/ppermute | solution.py:41
  14.6 0.0 copy-done.2
  14.6 1.9 %collective-permute-start.3 = (bf16[2,4,104,384]{3,2,1,0:T(8,128)(2,1)S(1)}, bf16[2,4,104,384]{3,2,1,0:T(8,128)(2,1)S(1)}, u32[]{:S(2)}, u32[]{:S(2)}) collective-permute-start(bf16[2,4,104,384]{3,2,1,0:T(8,128)(2,1)S(1)} %maximum_select_fusion.1.cells), channel_id=1, source_target_pairs={{0,16},{1,17},{2,18},{3,19},{4,20},{5,21},{6,22},{7,23},{8,24},{9,... | collective-permute-start | bytes 1916936 | tf_op jit(solution)/shard_map/ppermute | solution.py:41
  16.6 13.5 %collective-permute-done.1 = bf16[2,4,72,384]{3,2,1,0:T(8,128)(2,1)S(1)} collective-permute-done((bf16[2,4,72,384]{3,2,1,0:T(8,128)(2,1)S(1)}, bf16[2,4,72,384]{3,2,1,0:T(8,128)(2,1)S(1)}, u32[]{:S(2)}, u32[]{:S(2)}) %collective-permute-start.1) | collective-permute-done | bytes 442400 | tf_op jit(solution)/shard_map/ppermute | solution.py:41
  30.0 6.3 %collective-permute-start.2 = (bf16[2,4,72,384]{3,2,1,0:T(8,128)(2,1)S(1)}, bf16[2,4,72,384]{3,2,1,0:T(8,128)(2,1)S(1)}, u32[]{:S(2)}, u32[]{:S(2)}) collective-permute-start(bf16[2,4,72,384]{3,2,1,0:T(8,128)(2,1)S(1)} %collective-permute-done.1), channel_id=1, source_target_pairs={{48,32},{49,33},{50,34},{51,35},{52,36},{53,37},{54,38},{55,39},{5... | collective-permute-start | bytes 1327112 | tf_op jit(solution)/shard_map/ppermute | solution.py:41
  36.4 0.0 collective-permute-done.10.inner
  36.4 0.0 collective-permute-done.9.outer
  36.4 0.0 copy-start
  36.4 3.3 %copy-done = bf16[3,3,3,384,384]{4,3,2,1,0:T(8,128)(2,1)S(1)} copy-done((bf16[3,3,3,384,384]{4,3,2,1,0:T(8,128)(2,1)S(1)}, bf16[3,3,3,384,384]{4,3,2,1,0:T(8,128)(2,1)}, u32[]{:S(2)}) %copy-start) | copy-done | bytes 7962648
  39.7 6.3 %shard_map.46.own = f32[2,448,384]{2,1,0:T(8,128)S(1)} custom-call(s32[1]{0:T(128)} %bitcast.core, bf16[2,4,104,384]{3,2,1,0:T(8,128)(2,1)S(1)} %maximum_select_fusion.1.cells, bf16[2,1,104,384]{3,2,1,0:T(8,128)(2,1)S(1)} %collective-permute-done.9.outer, bf16[2,1,104,384]{3,2,1,0:T(8,128)(2,1)S(1)} %collective-permute-done.10.inner, ...), custom_call_target="tpu_custom_call" | custom-call | flops 10000000000 | bytes 10485760 | tf_op jit(solution)/shard_map/pallas_call | solution.py:147
  46.0 2.9 %collective-permute-done.3.cells = bf16[2,4,104,384]{3,2,1,0:T(8,128)(2,1)S(1)} collective-permute-done((bf16[2,4,104,384]{3,2,1,0:T(8,128)(2,1)S(1)}, bf16[2,4,104,384]{3,2,1,0:T(8,128)(2,1)S(1)}, u32[]{:S(2)}, u32[]{:S(2)}) %collective-permute-start.3) | collective-permute-done | bytes 639008 | tf_op jit(solution)/shard_map/ppermute | solution.py:41
  48.9 0.0 copy-start.1
  48.9 2.1 %collective-permute-start.4 = (bf16[2,4,32,384]{3,2,1,0:T(8,128)(2,1)S(1)}, bf16[2,4,32,384]{3,2,1,0:T(8,128)(2,1)S(1)}, u32[]{:S(2)}, u32[]{:S(2)}) collective-permute-start(bf16[2,4,32,384]{3,2,1,0:T(8,128)(2,1)S(1)} %slice.9), channel_id=1, source_target_pairs={{0,16},{1,17},{2,18},{3,19},{4,20},{5,21},{6,22},{7,23},{8,24},{9,... | collective-permute-start | bytes 589832 | tf_op jit(solution)/shard_map/ppermute | solution.py:41
  51.1 1.9 %collective-permute-start.7 = (bf16[2,1,104,384]{3,2,1,0:T(8,128)(2,1)S(1)}, bf16[2,1,104,384]{3,2,1,0:T(8,128)(2,1)S(1)}, u32[]{:S(2)}, u32[]{:S(2)}) collective-permute-start(bf16[2,1,104,384]{3,2,1,0:T(8,128)(2,1)S(1)} %get-tuple-element.16), channel_id=1, source_target_pairs={{1,8},{2,9},{3,10},{4,11},{5,12},{6,13},{7,14},{8,1},{9,2},{10,3},... | collective-permute-start | bytes 479240 | tf_op jit(solution)/shard_map/ppermute | solution.py:41
  53.0 6.8 %collective-permute-start.8 = (bf16[2,1,104,384]{3,2,1,0:T(8,128)(2,1)S(1)}, bf16[2,1,104,384]{3,2,1,0:T(8,128)(2,1)S(1)}, u32[]{:S(2)}, u32[]{:S(2)}) collective-permute-start(bf16[2,1,104,384]{3,2,1,0:T(8,128)(2,1)S(1)} %get-tuple-element.15), channel_id=1, source_target_pairs={{0,8},{1,9},{2,10},{3,11},{4,12},{5,13},{6,14},{7,15},{8,0},{9,1},... | collective-permute-start | bytes 479240 | tf_op jit(solution)/shard_map/ppermute | solution.py:41
  59.7 0.0 collective-permute-done.2
  59.8 0.1 collective-permute-done.4
  60.0 1.9 %collective-permute-start.5 = (bf16[2,1,104,384]{3,2,1,0:T(8,128)(2,1)S(1)}, bf16[2,1,104,384]{3,2,1,0:T(8,128)(2,1)S(1)}, u32[]{:S(2)}, u32[]{:S(2)}) collective-permute-start(bf16[2,1,104,384]{3,2,1,0:T(8,128)(2,1)S(1)} %get-tuple-element.18), channel_id=1, source_target_pairs={{1,8},{2,9},{3,10},{4,11},{5,12},{6,13},{7,14},{8,1},{9,2},{10,3},... | collective-permute-start | bytes 479240 | tf_op jit(solution)/shard_map/ppermute | solution.py:41
  61.9 9.2 %collective-permute-start.6 = (bf16[2,1,104,384]{3,2,1,0:T(8,128)(2,1)S(1)}, bf16[2,1,104,384]{3,2,1,0:T(8,128)(2,1)S(1)}, u32[]{:S(2)}, u32[]{:S(2)}) collective-permute-start(bf16[2,1,104,384]{3,2,1,0:T(8,128)(2,1)S(1)} %get-tuple-element.17), channel_id=1, source_target_pairs={{0,8},{1,9},{2,10},{3,11},{4,12},{5,13},{6,14},{7,15},{8,0},{9,1},... | collective-permute-start | bytes 479240 | tf_op jit(solution)/shard_map/ppermute | solution.py:41
  71.1 0.0 collective-permute-done.7.outer
  71.1 0.0 collective-permute-done.8.inner
  71.1 0.0 copy-done.1
  71.1 15.7 %shard_map.47 = (f32[2,448,384]{2,1,0:T(8,128)S(1)}, f32[2,448,768]{2,1,0:T(8,128)S(1)}) custom-call(s32[1]{0:T(128)} %bitcast.core, bf16[2,4,104,384]{3,2,1,0:T(8,128)(2,1)S(1)} %collective-permute-done.3.cells, bf16[2,1,104,384]{3,2,1,0:T(8,128)(2,1)S(1)} %collective-permute-done.7.outer, bf16[2,1,104,384]{3,2,1,0:T(8,128)(2,1)S(1)} %collective-permute-done.8.inner, ...), custom_call_target="tpu_custom_call" | custom-call | flops 20000000000 | bytes 10485760 | tf_op jit(solution)/shard_map/pallas_call | solution.py:147
  86.8 0.0 collective-permute-done.5.outer
  86.9 0.0 collective-permute-done.6.inner
  86.9 11.2 %shard_map.48 = (bf16[2,4,104,384]{3,2,1,0:T(8,128)(2,1)S(1)}, bf16[2,4,104,384]{3,2,1,0:T(8,128)(2,1)S(1)}) custom-call(s32[1]{0:T(128)} %bitcast.core, bf16[2,4,104,384]{3,2,1,0:T(8,128)(2,1)S(1)} %constant_dynamic-update-slice_fusion.cells, bf16[2,1,104,384]{3,2,1,0:T(8,128)(2,1)S(1)} %collective-permute-done.5.outer, ...), custom_call_target="tpu_custom_call" | custom-call | flops 10000000000 | bytes 10485760 | tf_op jit(solution)/shard_map/pallas_call | solution.py:147
  98.1 0.1 collective-permute-start.11
  98.2 2.0 %collective-permute-done.11 = bf16[2,4,104,384]{3,2,1,0:T(8,128)(2,1)S(1)} collective-permute-done((bf16[2,4,104,384]{3,2,1,0:T(8,128)(2,1)S(1)}, bf16[2,4,104,384]{3,2,1,0:T(8,128)(2,1)S(1)}, u32[]{:S(2)}, u32[]{:S(2)}) %collective-permute-start.11) | collective-permute-done | bytes 639008 | tf_op jit(solution)/shard_map/ppermute | solution.py:41
  100.2 1.3 %maximum_select_fusion = bf16[2,8,104,384]{3,2,1,0:T(8,128)(2,1)} fusion(bf16[2,4,104,384]{3,2,1,0:T(8,128)(2,1)S(1)} %collective-permute-done.11, bf16[2,4,104,384]{3,2,1,0:T(8,128)(2,1)S(1)} %get-tuple-element.11, pred[]{:T(512)S(6)} %eq.6), kind=kLoop, calls=%fused_computation | loop fusion | flops 1916928 | bytes 2555905 | tf_op jit(solution)/shard_map/jit(_where)/select_n | solution.py:214
  (8 shorter events, 0.3 us)
Async XLA Ops:
  1.1 2.0 %collective-permute-start = (bf16[1,4,104,384]{3,2,1,0:T(8,128)(2,1)S(1)}, bf16[1,4,104,384]{3,2,1,0:T(8,128)(2,1)S(1)}, u32[]{:S(2)}, u32[]{:S(2)}) collective-permute-start(bf16[1,4,104,384]{3,2,1,0:T(8,128)(2,1)S(1)} %get-tuple-element.20), channel_id=1, source_target_pairs={{0,8},{1,9},{2,10},{3,11},{4,12},{5,13},{6,14},{7,15},{8,0},{9,1},... | collective-permute-start | bytes 958472 | tf_op jit(solution)/shard_map/ppermute | solution.py:41
  3.1 11.5 %copy-start.2 = (f32[384]{0:T(512)S(1)}, f32[384]{0:T(512)}, u32[]{:S(2)}) copy-start(f32[384]{0:T(512)} %param.5) | copy-start | bytes 4612
  3.3 26.7 %collective-permute-start.1 = (bf16[2,4,72,384]{3,2,1,0:T(8,128)(2,1)S(1)}, bf16[2,4,72,384]{3,2,1,0:T(8,128)(2,1)S(1)}, u32[]{:S(2)}, u32[]{:S(2)}) collective-permute-start(bf16[2,4,72,384]{3,2,1,0:T(8,128)(2,1)S(1)} %slice.8), channel_id=1, source_target_pairs={{0,48},{1,49},{2,50},{3,51},{4,52},{5,53},{6,54},{7,55},{8,56},{9,... | collective-permute-start | bytes 1327112 | tf_op jit(solution)/shard_map/ppermute | solution.py:41
  11.3 25.1 %collective-permute-start.10 = (bf16[2,1,104,384]{3,2,1,0:T(8,128)(2,1)S(1)}, bf16[2,1,104,384]{3,2,1,0:T(8,128)(2,1)S(1)}, u32[]{:S(2)}, u32[]{:S(2)}) collective-permute-start(bf16[2,1,104,384]{3,2,1,0:T(8,128)(2,1)S(1)} %get-tuple-element.13), channel_id=1, source_target_pairs={{0,8},{1,9},{2,10},{3,11},{4,12},{5,13},{6,14},{7,15},{8,0},{9,1},... | collective-permute-start | bytes 479240 | tf_op jit(solution)/shard_map/ppermute | solution.py:41
  12.1 24.3 %collective-permute-start.9 = (bf16[2,1,104,384]{3,2,1,0:T(8,128)(2,1)S(1)}, bf16[2,1,104,384]{3,2,1,0:T(8,128)(2,1)S(1)}, u32[]{:S(2)}, u32[]{:S(2)}) collective-permute-start(bf16[2,1,104,384]{3,2,1,0:T(8,128)(2,1)S(1)} %get-tuple-element.14), channel_id=1, source_target_pairs={{1,8},{2,9},{3,10},{4,11},{5,12},{6,13},{7,14},{8,1},{9,2},{10,3},... | collective-permute-start | bytes 479240 | tf_op jit(solution)/shard_map/ppermute | solution.py:41
  14.6 34.3 %collective-permute-start.3 = (bf16[2,4,104,384]{3,2,1,0:T(8,128)(2,1)S(1)}, bf16[2,4,104,384]{3,2,1,0:T(8,128)(2,1)S(1)}, u32[]{:S(2)}, u32[]{:S(2)}) collective-permute-start(bf16[2,4,104,384]{3,2,1,0:T(8,128)(2,1)S(1)} %maximum_select_fusion.1.cells), channel_id=1, source_target_pairs={{0,16},{1,17},{2,18},{3,19},{4,20},{5,21},{6,22},{7,23},{8,24},{9,... | collective-permute-start | bytes 1916936 | tf_op jit(solution)/shard_map/ppermute | solution.py:41
  30.0 29.7 %collective-permute-start.2 = (bf16[2,4,72,384]{3,2,1,0:T(8,128)(2,1)S(1)}, bf16[2,4,72,384]{3,2,1,0:T(8,128)(2,1)S(1)}, u32[]{:S(2)}, u32[]{:S(2)}) collective-permute-start(bf16[2,4,72,384]{3,2,1,0:T(8,128)(2,1)S(1)} %collective-permute-done.1), channel_id=1, source_target_pairs={{48,32},{49,33},{50,34},{51,35},{52,36},{53,37},{54,38},{55,39},{5... | collective-permute-start | bytes 1327112 | tf_op jit(solution)/shard_map/ppermute | solution.py:41
  36.4 3.3 %copy-start = (bf16[3,3,3,384,384]{4,3,2,1,0:T(8,128)(2,1)S(1)}, bf16[3,3,3,384,384]{4,3,2,1,0:T(8,128)(2,1)}, u32[]{:S(2)}) copy-start(bf16[3,3,3,384,384]{4,3,2,1,0:T(8,128)(2,1)} %param.6) | copy-start | bytes 23887876
  48.9 22.2 %copy-start.1 = (bf16[3,384,768]{2,1,0:T(8,128)(2,1)S(1)}, bf16[3,384,768]{2,1,0:T(8,128)(2,1)}, u32[]{:S(2)}) copy-start(bf16[3,384,768]{2,1,0:T(8,128)(2,1)} %up.3) | copy-start | bytes 5308420
  48.9 11.0 %collective-permute-start.4 = (bf16[2,4,32,384]{3,2,1,0:T(8,128)(2,1)S(1)}, bf16[2,4,32,384]{3,2,1,0:T(8,128)(2,1)S(1)}, u32[]{:S(2)}, u32[]{:S(2)}) collective-permute-start(bf16[2,4,32,384]{3,2,1,0:T(8,128)(2,1)S(1)} %slice.9), channel_id=1, source_target_pairs={{0,16},{1,17},{2,18},{3,19},{4,20},{5,21},{6,22},{7,23},{8,24},{9,... | collective-permute-start | bytes 589832 | tf_op jit(solution)/shard_map/ppermute | solution.py:41
  51.1 20.0 %collective-permute-start.7 = (bf16[2,1,104,384]{3,2,1,0:T(8,128)(2,1)S(1)}, bf16[2,1,104,384]{3,2,1,0:T(8,128)(2,1)S(1)}, u32[]{:S(2)}, u32[]{:S(2)}) collective-permute-start(bf16[2,1,104,384]{3,2,1,0:T(8,128)(2,1)S(1)} %get-tuple-element.16), channel_id=1, source_target_pairs={{1,8},{2,9},{3,10},{4,11},{5,12},{6,13},{7,14},{8,1},{9,2},{10,3},... | collective-permute-start | bytes 479240 | tf_op jit(solution)/shard_map/ppermute | solution.py:41
  53.0 18.1 %collective-permute-start.8 = (bf16[2,1,104,384]{3,2,1,0:T(8,128)(2,1)S(1)}, bf16[2,1,104,384]{3,2,1,0:T(8,128)(2,1)S(1)}, u32[]{:S(2)}, u32[]{:S(2)}) collective-permute-start(bf16[2,1,104,384]{3,2,1,0:T(8,128)(2,1)S(1)} %get-tuple-element.15), channel_id=1, source_target_pairs={{0,8},{1,9},{2,10},{3,11},{4,12},{5,13},{6,14},{7,15},{8,0},{9,1},... | collective-permute-start | bytes 479240 | tf_op jit(solution)/shard_map/ppermute | solution.py:41
  60.0 26.8 %collective-permute-start.5 = (bf16[2,1,104,384]{3,2,1,0:T(8,128)(2,1)S(1)}, bf16[2,1,104,384]{3,2,1,0:T(8,128)(2,1)S(1)}, u32[]{:S(2)}, u32[]{:S(2)}) collective-permute-start(bf16[2,1,104,384]{3,2,1,0:T(8,128)(2,1)S(1)} %get-tuple-element.18), channel_id=1, source_target_pairs={{1,8},{2,9},{3,10},{4,11},{5,12},{6,13},{7,14},{8,1},{9,2},{10,3},... | collective-permute-start | bytes 479240 | tf_op jit(solution)/shard_map/ppermute | solution.py:41
  61.9 24.9 %collective-permute-start.6 = (bf16[2,1,104,384]{3,2,1,0:T(8,128)(2,1)S(1)}, bf16[2,1,104,384]{3,2,1,0:T(8,128)(2,1)S(1)}, u32[]{:S(2)}, u32[]{:S(2)}) collective-permute-start(bf16[2,1,104,384]{3,2,1,0:T(8,128)(2,1)S(1)} %get-tuple-element.17), channel_id=1, source_target_pairs={{0,8},{1,9},{2,10},{3,11},{4,12},{5,13},{6,14},{7,15},{8,0},{9,1},... | collective-permute-start | bytes 479240 | tf_op jit(solution)/shard_map/ppermute | solution.py:41
  98.1 2.2 %collective-permute-start.11 = (bf16[2,4,104,384]{3,2,1,0:T(8,128)(2,1)S(1)}, bf16[2,4,104,384]{3,2,1,0:T(8,128)(2,1)S(1)}, u32[]{:S(2)}, u32[]{:S(2)}) collective-permute-start(bf16[2,4,104,384]{3,2,1,0:T(8,128)(2,1)S(1)} %get-tuple-element.12), channel_id=1, source_target_pairs={{0,8},{1,9},{2,10},{3,11},{4,12},{5,13},{6,14},{7,15},{8,0},{9,1},... | collective-permute-start | bytes 1916936 | tf_op jit(solution)/shard_map/ppermute | solution.py:41

commit v2 on v1

v2 whole, which is shorter than its diff:
```python
import jax
import jax.numpy as jnp
from jax import lax
from jax.experimental import pallas as pl
from jax.experimental.pallas import tpu as pltpu
from jax.sharding import PartitionSpec as P

EPS = 1e-06
AXES = ("tm", "rows")
PAIRS = 16
BLOCKS = 8
PITCH = 112
CUT = 72


def device(pair, core, block):
    return (pair * 2 + core) * BLOCKS + block


def routes():
    every = [(m, c, r) for m in range(PAIRS) for c in range(2) for r in range(BLOCKS)]
    swap = [(device(m, c, r), device(m, 1 - c, r)) for m, c, r in every]
    ahead = [(device(m, c, r), device(m + 1, c, r)) for m, c, r in every if m + 1 < PAIRS]

    def back(m):
        return m // 4 * 4 + (m - 1) % 4

    far = [(m, c, r) for m, c, r in every if m + 2 < PAIRS]
    behind = [(device(m, c, r), device(back(m), c, r)) for m, c, r in far]
    behind_again = [(device(back(m), c, r), device(m + 2, c, r)) for m, c, r in far]
    edges = []
    for m, c, r in every:
        to = r + (1 if c else -1)
        if 0 <= to < BLOCKS:
            edges.append((device(m, c, r), device(m, 1 - c, to)))
    return swap, ahead, behind, behind_again, edges


def send(block, route):
    return lax.ppermute(block, AXES, route)


def dot(lhs, rhs):
    return jnp.dot(lhs, rhs, preferred_element_type=jnp.float32)


def columns_of(values, gain):
    values = values.astype(jnp.float32)
    scaled = values * lax.rsqrt(jnp.mean(values * values, axis=-1, keepdims=True) + EPS) * gain
    active = scaled / (1.0 + jnp.exp(-scaled))
    extra = jnp.zeros((PITCH - values.shape[0], values.shape[1]), jnp.float32)
    active = jnp.concatenate([active, extra], 0)
    shifts = (pltpu.roll(active, 1, 0), active, pltpu.roll(active, PITCH - 1, 0))
    return [shift.astype(jnp.bfloat16) for shift in shifts]


def fill_taps(row, gain, taps):
    rows, channels = taps.shape[1], taps.shape[3] // 9
    scale = gain[...]

    def frame(f, _):
        empty = [jnp.zeros((PITCH, channels), jnp.bfloat16)] * 3
        for q in range(rows + 2):
            inside = 0 < q <= rows
            columns = columns_of(row(f, q - 1), scale) if inside else empty
            for b in range(3):
                i = q - b
                if 0 <= i < rows:
                    for k in range(3):
                        start = (b * 3 + k) * channels
                        taps[f, i, :, start : start + channels] = columns[k]
        return 0

    lax.fori_loop(0, 2, frame, 0)


def product(taps, f, weight, *times):
    lhs = taps[f].reshape(-1, taps.shape[-1])
    return dot(lhs, jnp.concatenate([weight[a] for a in times], 1))


def late_terms(cells, taps, weight, total):
    rows, width, channels = cells.shape[1:]
    older = product(taps, 0, weight, 1, 2)
    total[0] = older[:, channels:]
    total[1] = older[:, :channels] + product(taps, 1, weight, 2)
    for f in range(2):
        for i in range(rows):
            total[f, i * PITCH : i * PITCH + width] += cells[f, i].astype(jnp.float32)


def early_terms(taps, weight, before, total):
    channels = weight.shape[2]
    newer = product(taps, 1, weight, 0, 1)
    total[1] = before[1] + newer[:, :channels]
    total[0] = before[0] + newer[:, channels:] + product(taps, 0, weight, 0)


def stage_own(cells, gain, source, total, weight, taps, done):
    copy = pltpu.make_async_copy(source, weight, done)
    copy.start()
    fill_taps(lambda f, i: cells[f, i], gain, taps)
    copy.wait()
    late_terms(cells, taps, weight, total)


def stage_middle(cells, gain, weight, own, own_total, total, taps):
    fill_taps(lambda f, i: cells[f, i], gain, taps)
    early_terms(taps, weight, own, own_total)
    late_terms(cells, taps, weight, total)


def stage_old(away, near, gain, weight, middle, total, taps):
    def row(f, i):
        return jnp.concatenate(
            [away[f, i].astype(jnp.float32), near[f, i].astype(jnp.float32)], 0
        )

    fill_taps(row, gain, taps)
    early_terms(taps, weight, middle, total)


def stage_last(
    core, outer, inner, outer_old, inner_old, gain, weight, up, own, middle, keep, give, edge, lines
):
    rows, width, channels = keep.shape[1:]
    scale = gain[...]
    first = core[0] == 0
    depth = 3 * channels

    def put(j, i, value):
        value = value.astype(jnp.bfloat16)
        for o in range(2):
            if 0 <= j - o < 3:
                start = (j - o) * channels
                lines[o, i * PITCH : (i + 1) * PITCH, start : start + channels] = value

    def total(j, i):
        return (middle, own)[j // 2][j % 2, i * PITCH : (i + 1) * PITCH]

    for j in range(4):
        for i in range(1, rows - 1):
            put(j, i, total(j, i))
    for top in (True, False):
        for frame in range(6):
            far, close = (outer_old, inner_old) if frame < 2 else (outer, inner)
            f = frame if frame < 2 else frame - 2
            pair = (far[f, 0], close[f, 0]) if top else (close[f, 0], far[f, 0])
            columns = columns_of(jnp.where(first, *pair), scale)
            for a in range(3):
                j = frame - a
                if 0 <= j < 4:
                    for k in range(3):
                        start = a * depth + k * channels
                        edge[j * PITCH : (j + 1) * PITCH, start : start + channels] = columns[k]
        b = 0 if top else 2
        part = [weight[a, b * depth : (b + 1) * depth] for a in range(3)]
        value = dot(edge[...], jnp.concatenate(part, 0))
        i = 0 if top else rows - 1
        for j in range(4):
            put(j, i, total(j, i) + value[j * PITCH : (j + 1) * PITCH])

    def write(target, value):
        for k in range(2):
            for i in range(rows):
                piece = value[i * PITCH : i * PITCH + width, k * channels : (k + 1) * channels]
                target[k, i] = piece.astype(jnp.bfloat16)

    even = dot(lines[0], up[...])
    odd = dot(lines[1], up[...])

    @pl.when(first)
    def _():
        write(keep, even)
        write(give, odd)

    @pl.when(jnp.logical_not(first))
    def _():
        write(keep, odd)
        write(give, even)


VMEM = pl.BlockSpec(memory_space=pltpu.VMEM)
SMEM = pl.BlockSpec(memory_space=pltpu.SMEM)
ANY = pl.BlockSpec(memory_space=pl.ANY)


def call(body, outs, flops, args, specs, scratch):
    return pl.pallas_call(
        body,
        out_shape=outs,
        in_specs=[specs.get(n, VMEM) for n in range(len(args))],
        out_specs=[VMEM] * len(outs),
        scratch_shapes=scratch,
        compiler_params=pltpu.CompilerParams(vmem_limit_bytes=32 << 20),
        cost_estimate=pl.CostEstimate(flops=flops, bytes_accessed=1 << 20, transcendentals=0),
    )(*args)


def local(latents, norm_gain, conv_weight, up_weight):
    swap, ahead, behind, behind_again, edges = routes()
    core = lax.axis_index("tm") % 2
    rows, width, channels = latents.shape[1] // 2, latents.shape[2], latents.shape[3]
    gain = norm_gain.reshape(1, channels)
    weight = conv_weight.reshape(3, 9 * channels, channels)
    up = up_weight.reshape(3 * channels, 2 * channels)
    mark = core.reshape(1).astype(jnp.int32)
    size = rows * PITCH
    taps = pltpu.VMEM((2, rows, PITCH, 9 * channels), jnp.bfloat16)
    totals = jax.ShapeDtypeStruct((2, size, channels), jnp.float32)
    half = jax.ShapeDtypeStruct((2, rows, width, channels), jnp.bfloat16)

    kept = lax.dynamic_slice_in_dim(latents, core * rows, rows, 1)
    given = lax.dynamic_slice_in_dim(latents, (1 - core) * rows, rows, 1)
    taken = send(given, swap)
    own = jnp.where(
        core == 0, jnp.concatenate([kept, taken], 0), jnp.concatenate([taken, kept], 0)
    )

    def outer(pair):
        return lax.dynamic_slice_in_dim(pair, core * (rows - 1), 1, 1)

    def inner(pair):
        return lax.dynamic_slice_in_dim(pair, (1 - core) * (rows - 1), 1, 1)

    middle = send(own, ahead)
    away = send(own[:, :, :CUT], behind)
    own_total, held = call(
        stage_own,
        [totals, jax.ShapeDtypeStruct(weight.shape, weight.dtype)],
        5 * 10**9,
        (own, gain, weight),
        {2: ANY},
        [taps, pltpu.SemaphoreType.DMA],
    )
    away, own_total = lax.optimization_barrier((away, own_total))
    away = send(away, behind_again)
    middle, own_total = lax.optimization_barrier((middle, own_total))
    both = jnp.concatenate([middle, own], 0)
    outer_near, inner_near = send(outer(both), edges), send(inner(both), swap)
    near = send(middle[:, :, CUT:], ahead)
    own_total, middle_total = call(
        stage_middle, [totals, totals], 10**10, (middle, gain, held, own_total), {}, [taps]
    )
    away, near, middle_total = lax.optimization_barrier((away, near, middle_total))

    def joined(pick):
        return jnp.concatenate([pick(away), pick(near)], 2)

    outer_old, inner_old = send(joined(outer), edges), send(joined(inner), swap)
    (middle_total,) = call(
        stage_old, [totals], 5 * 10**9, (away, near, gain, held, middle_total), {}, [taps]
    )
    keep, give = call(
        stage_last,
        [half, half],
        5 * 10**9,
        (mark, outer_near, inner_near, outer_old, inner_old, gain, held, up, own_total, middle_total),
        {0: SMEM},
        [
            pltpu.VMEM((size, 9 * channels), jnp.bfloat16),
            pltpu.VMEM((2, size, 3 * channels), jnp.bfloat16),
        ],
    )
    got = send(give, swap)
    return jnp.where(
        core == 0, jnp.concatenate([keep, got], 1), jnp.concatenate([got, keep], 1)
    )


def solution(mesh):
    placed = (P("tm", "rows", None, None), P(), P(), P())
    return jax.shard_map(
        local, mesh=mesh, in_specs=placed, out_specs=P("tm", "rows", None, None), check_vma=False
    )
```

time: 103 us -> 80.4 us (0.78); the launches traced: 102 us -> 80.1 us
  starting transfers between devices: 42.2 us -> 32.3 us
  Pallas kernels: 33.2 us -> 26.7 us
  waiting for transfers between devices: 19.8 us -> 14.7 us
    ppermute x12 -> x10, starting transfers between devices: 42.2 us -> 32.3 us  [send(): return lax.ppermute(block, AXES, route)]
    pallas_call x3 -> x4, Pallas kernels: 33.2 us -> 26.7 us  [call(): pl.pallas_call(body, out_shape=outs, in_specs=[specs.get(n, VMEM) for n i...]
    ppermute x12 -> x10, waiting for transfers between devices: 19.8 us -> 14.7 us  [send(): return lax.ppermute(block, AXES, route)]
    unnamed x7 -> x6, local copies, waits for them, and re-layouts: 3.31 us -> 3.27 us
  transfers between devices with their start and end apart: 12 -> 10, of which waited for: 5 -> 4; matrix products, arithmetic and copies ran while one was open for 0% -> 0% of each run, Pallas kernels for 22% -> 26%
where the time goes in v2:
time: 80.4 us; the launch traced here: 80.1 us
  starting transfers between devices  32.3 us (40%)
  Pallas kernels  26.7 us (33%)
  waiting for transfers between devices  14.7 us (18%)
  local copies, waits for them, and re-layouts  4.53 us (6%)
  other arithmetic  1.57 us (2%)
    ppermute x10, starting transfers between devices, send(): return lax.ppermute(block, AXES, route)  32.3 us
    pallas_call x4, Pallas kernels, call(): pl.pallas_call(body, out_shape=outs, in_specs=[specs.get(n, VMEM) for n i...  26.7 us
    ppermute x10, waiting for transfers between devices, send(): return lax.ppermute(block, AXES, route)  14.7 us
    unnamed x6, local copies, waits for them, and re-layouts  3.27 us
  transfers between devices with their start and end apart: 10, of which 4 were waited for; matrix products, arithmetic and copies ran while one was open for 0% of the time, Pallas kernels for 26%

profile of v2, /device:TPU:29, one launch (start us, length us, event | category | flops | bytes accessed | tf_op | source)
XLA Modules:
  0.0 80.1 jit_solution(505506627077082021)
XLA Ops:
  0.0 0.0 copy-start.2
  0.0 1.1 %constant_dynamic-slice_fusion.5 = (bf16[1,4,104,384]{3,2,1,0:T(8,128)(2,1)S(1)}, bf16[1,4,104,384]{3,2,1,0:T(8,128)(2,1)S(1)}) fusion(bf16[1,8,104,384]{3,2,1,0:T(8,128)(2,1)} %param.4, s32[]{:T(128)S(6)} %select_n.42, s32[]{:T(128)S(6)} %select_n.43), kind=kLoop, calls=%fused_computation.15 | loop fusion | bytes 1277960 | tf_op jit(solution)/shard_map/dynamic_slice | solution.py:213
  1.1 0.8 collective-permute-start
  1.9 1.2 %collective-permute-done = bf16[1,4,104,384]{3,2,1,0:T(8,128)(2,1)S(1)} collective-permute-done((bf16[1,4,104,384]{3,2,1,0:T(8,128)(2,1)S(1)}, bf16[1,4,104,384]{3,2,1,0:T(8,128)(2,1)S(1)}, u32[]{:S(2)}, u32[]{:S(2)}) %collective-permute-start) | collective-permute-done | bytes 319520 | tf_op jit(solution)/shard_map/ppermute | solution.py:40
  3.2 0.1 maximum_select_fusion.1.cells
  3.3 4.9 %collective-permute-start.1 = (bf16[2,4,104,384]{3,2,1,0:T(8,128)(2,1)S(1)}, bf16[2,4,104,384]{3,2,1,0:T(8,128)(2,1)S(1)}, u32[]{:S(2)}, u32[]{:S(2)}) collective-permute-start(bf16[2,4,104,384]{3,2,1,0:T(8,128)(2,1)S(1)} %maximum_select_fusion.1.cells), channel_id=1, source_target_pairs={{0,16},{1,17},{2,18},{3,19},{4,20},{5,21},{6,22},{7,23},{8,24},{9,... | collective-permute-start | bytes 1916936 | tf_op jit(solution)/shard_map/ppermute | solution.py:40
  8.2 0.0 copy-done.2
  8.3 5.0 %collective-permute-start.2 = (bf16[2,4,72,384]{3,2,1,0:T(8,128)(2,1)S(1)}, bf16[2,4,72,384]{3,2,1,0:T(8,128)(2,1)S(1)}, u32[]{:S(2)}, u32[]{:S(2)}) collective-permute-start(bf16[2,4,72,384]{3,2,1,0:T(8,128)(2,1)S(1)} %slice.8), channel_id=1, source_target_pairs={{0,48},{1,49},{2,50},{3,51},{4,52},{5,53},{6,54},{7,55},{8,56},{9,... | collective-permute-start | bytes 1327112 | tf_op jit(solution)/shard_map/ppermute | solution.py:40
  13.2 0.0 copy-start
  13.3 3.3 %copy-done = bf16[3,3,3,384,384]{4,3,2,1,0:T(8,128)(2,1)S(1)} copy-done((bf16[3,3,3,384,384]{4,3,2,1,0:T(8,128)(2,1)S(1)}, bf16[3,3,3,384,384]{4,3,2,1,0:T(8,128)(2,1)}, u32[]{:S(2)}) %copy-start) | copy-done | bytes 7962648
  16.5 6.0 %shard_map.46 = (f32[2,448,384]{2,1,0:T(8,128)S(1)}, bf16[3,3456,384]{2,1,0:T(8,128)(2,1)S(1)}) custom-call(bf16[2,4,104,384]{3,2,1,0:T(8,128)(2,1)S(1)} %maximum_select_fusion.1.cells, f32[1,384]{1,0:T(1,128)S(1)} %reshape.13.gain, bf16[3,3456,384]{2,1,0:T(8,128)(2,1)S(1)} %bitcast.3), custom_call_target="tpu_custom_call" | custom-call | flops 5000000000 | bytes 1048576 | tf_op jit(solution)/shard_map/pallas_call | solution.py:189
  22.5 11.6 %collective-permute-done.2 = bf16[2,4,72,384]{3,2,1,0:T(8,128)(2,1)S(1)} collective-permute-done((bf16[2,4,72,384]{3,2,1,0:T(8,128)(2,1)S(1)}, bf16[2,4,72,384]{3,2,1,0:T(8,128)(2,1)S(1)}, u32[]{:S(2)}, u32[]{:S(2)}) %collective-permute-start.2) | collective-permute-done | bytes 442400 | tf_op jit(solution)/shard_map/ppermute | solution.py:40
  34.1 4.3 %collective-permute-start.5 = (bf16[2,4,72,384]{3,2,1,0:T(8,128)(2,1)S(1)}, bf16[2,4,72,384]{3,2,1,0:T(8,128)(2,1)S(1)}, u32[]{:S(2)}, u32[]{:S(2)}) collective-permute-start(bf16[2,4,72,384]{3,2,1,0:T(8,128)(2,1)S(1)} %collective-permute-done.2), channel_id=1, source_target_pairs={{48,32},{49,33},{50,34},{51,35},{52,36},{53,37},{54,38},{55,39},{5... | collective-permute-start | bytes 1327112 | tf_op jit(solution)/shard_map/ppermute | solution.py:40
  38.4 0.0 collective-permute-done.1.cells
  38.4 3.2 %collective-permute-start.6 = (bf16[2,4,32,384]{3,2,1,0:T(8,128)(2,1)S(1)}, bf16[2,4,32,384]{3,2,1,0:T(8,128)(2,1)S(1)}, u32[]{:S(2)}, u32[]{:S(2)}) collective-permute-start(bf16[2,4,32,384]{3,2,1,0:T(8,128)(2,1)S(1)} %slice.7), channel_id=1, source_target_pairs={{0,16},{1,17},{2,18},{3,19},{4,20},{5,21},{6,22},{7,23},{8,24},{9,... | collective-permute-start | bytes 589832 | tf_op jit(solution)/shard_map/ppermute | solution.py:40
  41.7 0.1 fusion
  41.8 5.4 %collective-permute-start.3 = (bf16[4,1,104,384]{3,2,1,0:T(8,128)(2,1)S(1)}, bf16[4,1,104,384]{3,2,1,0:T(8,128)(2,1)S(1)}, u32[]{:S(2)}, u32[]{:S(2)}) collective-permute-start(bf16[4,1,104,384]{3,2,1,0:T(8,128)(2,1)S(1)} %get-tuple-element.32), channel_id=1, source_target_pairs={{1,8},{2,9},{3,10},{4,11},{5,12},{6,13},{7,14},{8,1},{9,2},{10,3},... | collective-permute-start | bytes 958472 | tf_op jit(solution)/shard_map/ppermute | solution.py:40
  47.2 0.1 collective-permute-start.4
  47.3 9.4 %shard_map.47 = (f32[2,448,384]{2,1,0:T(8,128)S(1)}, f32[2,448,384]{2,1,0:T(8,128)S(1)}) custom-call(bf16[2,4,104,384]{3,2,1,0:T(8,128)(2,1)S(1)} %collective-permute-done.1.cells, f32[1,384]{1,0:T(1,128)S(1)} %reshape.13.gain, bf16[3,3456,384]{2,1,0:T(8,128)(2,1)S(1)} %get-tuple-element.22.weight, f32[2,448,384]{2,1,0:T(8,128)S(1)} %get-tuple-element.23.own), custom_call_target="tpu_custom_call" | custom-call | flops 10000000000 | bytes 1048576 | tf_op jit(solution)/shard_map/pallas_call | solution.py:189
  56.7 0.0 collective-permute-done.6.near
  56.7 0.2 collective-permute-done.5.away
  57.0 3.4 %collective-permute-start.8 = (bf16[2,1,104,384]{3,2,1,0:T(8,128)(2,1)S(1)}, bf16[2,1,104,384]{3,2,1,0:T(8,128)(2,1)S(1)}, u32[]{:S(2)}, u32[]{:S(2)}) collective-permute-start(bf16[2,1,104,384]{3,2,1,0:T(8,128)(2,1)S(1)} %pad_maximum_fusion.1), channel_id=1, source_target_pairs={{0,8},{1,9},{2,10},{3,11},{4,12},{5,13},{6,14},{7,15},{8,0},{9,1},... | collective-permute-start | bytes 479240 | tf_op jit(solution)/shard_map/ppermute | solution.py:40
  60.4 0.0 copy-start.1
  60.4 2.2 %collective-permute-start.7 = (bf16[2,1,104,384]{3,2,1,0:T(8,128)(2,1)S(1)}, bf16[2,1,104,384]{3,2,1,0:T(8,128)(2,1)S(1)}, u32[]{:S(2)}, u32[]{:S(2)}) collective-permute-start(bf16[2,1,104,384]{3,2,1,0:T(8,128)(2,1)S(1)} %pad_maximum_fusion), channel_id=1, source_target_pairs={{1,8},{2,9},{3,10},{4,11},{5,12},{6,13},{7,14},{8,1},{9,2},{10,3},... | collective-permute-start | bytes 479240 | tf_op jit(solution)/shard_map/ppermute | solution.py:40
  62.6 5.3 %shard_map.48.middle = f32[2,448,384]{2,1,0:T(8,128)S(1)} custom-call(bf16[2,4,72,384]{3,2,1,0:T(8,128)(2,1)S(1)} %collective-permute-done.5.away, bf16[2,4,32,384]{3,2,1,0:T(8,128)(2,1)S(1)} %collective-permute-done.6.near, f32[1,384]{1,0:T(1,128)S(1)} %reshape.13.gain, bf16[3,3456,384]{2,1,0:T(8,128)(2,1)S(1)} %get-tuple-element.22.weight, ...), custom_call_target="tpu_custom_call" | custom-call | flops 5000000000 | bytes 1048576 | tf_op jit(solution)/shard_map/pallas_call | solution.py:189
  67.9 0.0 collective-permute-done.3.outer
  67.9 0.0 collective-permute-done.4.inner
  67.9 0.0 collective-permute-done.8.inner_old
  67.9 0.0 collective-permute-done.7.outer_old
  67.9 0.0 copy-done.1
  67.9 6.0 %shard_map.49 = (bf16[2,4,104,384]{3,2,1,0:T(8,128)(2,1)S(1)}, bf16[2,4,104,384]{3,2,1,0:T(8,128)(2,1)S(1)}) custom-call(s32[1]{0:T(128)} %bitcast.core, bf16[4,1,104,384]{3,2,1,0:T(8,128)(2,1)S(1)} %collective-permute-done.3.outer, bf16[4,1,104,384]{3,2,1,0:T(8,128)(2,1)S(1)} %collective-permute-done.4.inner, ...), custom_call_target="tpu_custom_call" | custom-call | flops 5000000000 | bytes 1048576 | tf_op jit(solution)/shard_map/pallas_call | solution.py:189
  74.0 3.0 %collective-permute-start.9 = (bf16[2,4,104,384]{3,2,1,0:T(8,128)(2,1)S(1)}, bf16[2,4,104,384]{3,2,1,0:T(8,128)(2,1)S(1)}, u32[]{:S(2)}, u32[]{:S(2)}) collective-permute-start(bf16[2,4,104,384]{3,2,1,0:T(8,128)(2,1)S(1)} %get-tuple-element.30), channel_id=1, source_target_pairs={{0,8},{1,9},{2,10},{3,11},{4,12},{5,13},{6,14},{7,15},{8,0},{9,1},... | collective-permute-start | bytes 1916936 | tf_op jit(solution)/shard_map/ppermute | solution.py:40
  77.0 1.7 %collective-permute-done.9 = bf16[2,4,104,384]{3,2,1,0:T(8,128)(2,1)S(1)} collective-permute-done((bf16[2,4,104,384]{3,2,1,0:T(8,128)(2,1)S(1)}, bf16[2,4,104,384]{3,2,1,0:T(8,128)(2,1)S(1)}, u32[]{:S(2)}, u32[]{:S(2)}) %collective-permute-start.9) | collective-permute-done | bytes 639008 | tf_op jit(solution)/shard_map/ppermute | solution.py:40
  78.8 1.3 %maximum_select_fusion = bf16[2,8,104,384]{3,2,1,0:T(8,128)(2,1)} fusion(bf16[2,4,104,384]{3,2,1,0:T(8,128)(2,1)S(1)} %collective-permute-done.9, bf16[2,4,104,384]{3,2,1,0:T(8,128)(2,1)S(1)} %get-tuple-element.29, pred[]{:T(512)S(6)} %eq.6), kind=kLoop, calls=%fused_computation.4 | loop fusion | flops 1916928 | bytes 2555905 | tf_op jit(solution)/shard_map/jit(_where)/select_n | solution.py:266
  (7 shorter events, 0.2 us)
Async XLA Ops:
  0.0 8.2 %copy-start.2 = (f32[384]{0:T(512)S(1)}, f32[384]{0:T(512)}, u32[]{:S(2)}) copy-start(f32[384]{0:T(512)} %param.5) | copy-start | bytes 4612
  1.1 2.0 %collective-permute-start = (bf16[1,4,104,384]{3,2,1,0:T(8,128)(2,1)S(1)}, bf16[1,4,104,384]{3,2,1,0:T(8,128)(2,1)S(1)}, u32[]{:S(2)}, u32[]{:S(2)}) collective-permute-start(bf16[1,4,104,384]{3,2,1,0:T(8,128)(2,1)S(1)} %get-tuple-element.34), channel_id=1, source_target_pairs={{0,8},{1,9},{2,10},{3,11},{4,12},{5,13},{6,14},{7,15},{8,0},{9,1},... | collective-permute-start | bytes 958472 | tf_op jit(solution)/shard_map/ppermute | solution.py:40
  3.3 35.1 %collective-permute-start.1 = (bf16[2,4,104,384]{3,2,1,0:T(8,128)(2,1)S(1)}, bf16[2,4,104,384]{3,2,1,0:T(8,128)(2,1)S(1)}, u32[]{:S(2)}, u32[]{:S(2)}) collective-permute-start(bf16[2,4,104,384]{3,2,1,0:T(8,128)(2,1)S(1)} %maximum_select_fusion.1.cells), channel_id=1, source_target_pairs={{0,16},{1,17},{2,18},{3,19},{4,20},{5,21},{6,22},{7,23},{8,24},{9,... | collective-permute-start | bytes 1916936 | tf_op jit(solution)/shard_map/ppermute | solution.py:40
  8.3 25.8 %collective-permute-start.2 = (bf16[2,4,72,384]{3,2,1,0:T(8,128)(2,1)S(1)}, bf16[2,4,72,384]{3,2,1,0:T(8,128)(2,1)S(1)}, u32[]{:S(2)}, u32[]{:S(2)}) collective-permute-start(bf16[2,4,72,384]{3,2,1,0:T(8,128)(2,1)S(1)} %slice.8), channel_id=1, source_target_pairs={{0,48},{1,49},{2,50},{3,51},{4,52},{5,53},{6,54},{7,55},{8,56},{9,... | collective-permute-start | bytes 1327112 | tf_op jit(solution)/shard_map/ppermute | solution.py:40
  13.2 3.3 %copy-start = (bf16[3,3,3,384,384]{4,3,2,1,0:T(8,128)(2,1)S(1)}, bf16[3,3,3,384,384]{4,3,2,1,0:T(8,128)(2,1)}, u32[]{:S(2)}) copy-start(bf16[3,3,3,384,384]{4,3,2,1,0:T(8,128)(2,1)} %param.6) | copy-start | bytes 23887876
  34.1 22.8 %collective-permute-start.5 = (bf16[2,4,72,384]{3,2,1,0:T(8,128)(2,1)S(1)}, bf16[2,4,72,384]{3,2,1,0:T(8,128)(2,1)S(1)}, u32[]{:S(2)}, u32[]{:S(2)}) collective-permute-start(bf16[2,4,72,384]{3,2,1,0:T(8,128)(2,1)S(1)} %collective-permute-done.2), channel_id=1, source_target_pairs={{48,32},{49,33},{50,34},{51,35},{52,36},{53,37},{54,38},{55,39},{5... | collective-permute-start | bytes 1327112 | tf_op jit(solution)/shard_map/ppermute | solution.py:40
  38.4 18.3 %collective-permute-start.6 = (bf16[2,4,32,384]{3,2,1,0:T(8,128)(2,1)S(1)}, bf16[2,4,32,384]{3,2,1,0:T(8,128)(2,1)S(1)}, u32[]{:S(2)}, u32[]{:S(2)}) collective-permute-start(bf16[2,4,32,384]{3,2,1,0:T(8,128)(2,1)S(1)} %slice.7), channel_id=1, source_target_pairs={{0,16},{1,17},{2,18},{3,19},{4,20},{5,21},{6,22},{7,23},{8,24},{9,... | collective-permute-start | bytes 589832 | tf_op jit(solution)/shard_map/ppermute | solution.py:40
  41.8 26.1 %collective-permute-start.3 = (bf16[4,1,104,384]{3,2,1,0:T(8,128)(2,1)S(1)}, bf16[4,1,104,384]{3,2,1,0:T(8,128)(2,1)S(1)}, u32[]{:S(2)}, u32[]{:S(2)}) collective-permute-start(bf16[4,1,104,384]{3,2,1,0:T(8,128)(2,1)S(1)} %get-tuple-element.32), channel_id=1, source_target_pairs={{1,8},{2,9},{3,10},{4,11},{5,12},{6,13},{7,14},{8,1},{9,2},{10,3},... | collective-permute-start | bytes 958472 | tf_op jit(solution)/shard_map/ppermute | solution.py:40
  47.2 20.7 %collective-permute-start.4 = (bf16[4,1,104,384]{3,2,1,0:T(8,128)(2,1)S(1)}, bf16[4,1,104,384]{3,2,1,0:T(8,128)(2,1)S(1)}, u32[]{:S(2)}, u32[]{:S(2)}) collective-permute-start(bf16[4,1,104,384]{3,2,1,0:T(8,128)(2,1)S(1)} %get-tuple-element.31), channel_id=1, source_target_pairs={{0,8},{1,9},{2,10},{3,11},{4,12},{5,13},{6,14},{7,15},{8,0},{9,1},... | collective-permute-start | bytes 958472 | tf_op jit(solution)/shard_map/ppermute | solution.py:40
  57.0 10.9 %collective-permute-start.8 = (bf16[2,1,104,384]{3,2,1,0:T(8,128)(2,1)S(1)}, bf16[2,1,104,384]{3,2,1,0:T(8,128)(2,1)S(1)}, u32[]{:S(2)}, u32[]{:S(2)}) collective-permute-start(bf16[2,1,104,384]{3,2,1,0:T(8,128)(2,1)S(1)} %pad_maximum_fusion.1), channel_id=1, source_target_pairs={{0,8},{1,9},{2,10},{3,11},{4,12},{5,13},{6,14},{7,15},{8,0},{9,1},... | collective-permute-start | bytes 479240 | tf_op jit(solution)/shard_map/ppermute | solution.py:40
  60.4 7.6 %copy-start.1 = (bf16[3,384,768]{2,1,0:T(8,128)(2,1)S(1)}, bf16[3,384,768]{2,1,0:T(8,128)(2,1)}, u32[]{:S(2)}) copy-start(bf16[3,384,768]{2,1,0:T(8,128)(2,1)} %param.7) | copy-start | bytes 5308420
  60.4 7.6 %collective-permute-start.7 = (bf16[2,1,104,384]{3,2,1,0:T(8,128)(2,1)S(1)}, bf16[2,1,104,384]{3,2,1,0:T(8,128)(2,1)S(1)}, u32[]{:S(2)}, u32[]{:S(2)}) collective-permute-start(bf16[2,1,104,384]{3,2,1,0:T(8,128)(2,1)S(1)} %pad_maximum_fusion), channel_id=1, source_target_pairs={{1,8},{2,9},{3,10},{4,11},{5,12},{6,13},{7,14},{8,1},{9,2},{10,3},... | collective-permute-start | bytes 479240 | tf_op jit(solution)/shard_map/ppermute | solution.py:40
  74.0 4.8 %collective-permute-start.9 = (bf16[2,4,104,384]{3,2,1,0:T(8,128)(2,1)S(1)}, bf16[2,4,104,384]{3,2,1,0:T(8,128)(2,1)S(1)}, u32[]{:S(2)}, u32[]{:S(2)}) collective-permute-start(bf16[2,4,104,384]{3,2,1,0:T(8,128)(2,1)S(1)} %get-tuple-element.30), channel_id=1, source_target_pairs={{0,8},{1,9},{2,10},{3,11},{4,12},{5,13},{6,14},{7,15},{8,0},{9,1},... | collective-permute-start | bytes 1916936 | tf_op jit(solution)/shard_map/ppermute | solution.py:40

commit v3 on v2

--- a/solution.py
+++ b/solution.py
@@ -10,7 +10,7 @@
 PAIRS = 16
 BLOCKS = 8
 PITCH = 112
-CUT = 72
+CUT = 64
 
 
 def device(pair, core, block):

time: 80.4 us -> 78.9 us (0.981)
  waiting for transfers between devices: 14.7 us -> 12.4 us
    ppermute x10, waiting for transfers between devices: 14.7 us -> 12.4 us  [send(): return lax.ppermute(block, AXES, route)]
  transfers between devices with their start and end apart: 10 -> 10, of which waited for: 4 -> 3; matrix products, arithmetic and copies ran while one was open for 0% -> 0% of each run, Pallas kernels for 26% -> 27%
where the time goes in v3:
time: 78.9 us; the launch traced here: 78.6 us
  starting transfers between devices  32.8 us (42%)
  Pallas kernels  27.1 us (34%)
  waiting for transfers between devices  12.4 us (16%)
  local copies, waits for them, and re-layouts  4.53 us (6%)
  other arithmetic  1.57 us (2%)
    ppermute x10, starting transfers between devices, send(): return lax.ppermute(block, AXES, route)  32.8 us
    pallas_call x4, Pallas kernels, call(): pl.pallas_call(body, out_shape=outs, in_specs=[specs.get(n, VMEM) for n i...  27.1 us
    ppermute x10, waiting for transfers between devices, send(): return lax.ppermute(block, AXES, route)  12.4 us
    unnamed x6, local copies, waits for them, and re-layouts  3.27 us
  transfers between devices with their start and end apart: 10, of which 3 were waited for; matrix products, arithmetic and copies ran while one was open for 0% of the time, Pallas kernels for 27%

profile of v3, /device:TPU:29, one launch (start us, length us, event | category | flops | bytes accessed | tf_op | source)
XLA Modules:
  0.0 78.6 jit_solution(9741104425579275743)
XLA Ops:
  0.0 0.0 copy-start.2
  0.0 1.1 %constant_dynamic-slice_fusion.5 = (bf16[1,4,104,384]{3,2,1,0:T(8,128)(2,1)S(1)}, bf16[1,4,104,384]{3,2,1,0:T(8,128)(2,1)S(1)}) fusion(bf16[1,8,104,384]{3,2,1,0:T(8,128)(2,1)} %param.4, s32[]{:T(128)S(6)} %select_n.42, s32[]{:T(128)S(6)} %select_n.43), kind=kLoop, calls=%fused_computation.15 | loop fusion | bytes 1277960 | tf_op jit(solution)/shard_map/dynamic_slice | solution.py:213
  1.1 0.8 collective-permute-start
  1.9 1.2 %collective-permute-done = bf16[1,4,104,384]{3,2,1,0:T(8,128)(2,1)S(1)} collective-permute-done((bf16[1,4,104,384]{3,2,1,0:T(8,128)(2,1)S(1)}, bf16[1,4,104,384]{3,2,1,0:T(8,128)(2,1)S(1)}, u32[]{:S(2)}, u32[]{:S(2)}) %collective-permute-start) | collective-permute-done | bytes 319520 | tf_op jit(solution)/shard_map/ppermute | solution.py:40
  3.2 0.1 maximum_select_fusion.1.cells
  3.3 4.9 %collective-permute-start.1 = (bf16[2,4,104,384]{3,2,1,0:T(8,128)(2,1)S(1)}, bf16[2,4,104,384]{3,2,1,0:T(8,128)(2,1)S(1)}, u32[]{:S(2)}, u32[]{:S(2)}) collective-permute-start(bf16[2,4,104,384]{3,2,1,0:T(8,128)(2,1)S(1)} %maximum_select_fusion.1.cells), channel_id=1, source_target_pairs={{0,16},{1,17},{2,18},{3,19},{4,20},{5,21},{6,22},{7,23},{8,24},{9,... | collective-permute-start | bytes 1916936 | tf_op jit(solution)/shard_map/ppermute | solution.py:40
  8.2 0.0 copy-done.2
  8.3 5.0 %collective-permute-start.2 = (bf16[2,4,64,384]{3,2,1,0:T(8,128)(2,1)S(1)}, bf16[2,4,64,384]{3,2,1,0:T(8,128)(2,1)S(1)}, u32[]{:S(2)}, u32[]{:S(2)}) collective-permute-start(bf16[2,4,64,384]{3,2,1,0:T(8,128)(2,1)S(1)} %slice.8), channel_id=1, source_target_pairs={{0,48},{1,49},{2,50},{3,51},{4,52},{5,53},{6,54},{7,55},{8,56},{9,... | collective-permute-start | bytes 1179656 | tf_op jit(solution)/shard_map/ppermute | solution.py:40
  13.2 0.0 copy-start
  13.3 3.3 %copy-done = bf16[3,3,3,384,384]{4,3,2,1,0:T(8,128)(2,1)S(1)} copy-done((bf16[3,3,3,384,384]{4,3,2,1,0:T(8,128)(2,1)S(1)}, bf16[3,3,3,384,384]{4,3,2,1,0:T(8,128)(2,1)}, u32[]{:S(2)}) %copy-start) | copy-done | bytes 7962648
  16.5 6.0 %shard_map.46 = (f32[2,448,384]{2,1,0:T(8,128)S(1)}, bf16[3,3456,384]{2,1,0:T(8,128)(2,1)S(1)}) custom-call(bf16[2,4,104,384]{3,2,1,0:T(8,128)(2,1)S(1)} %maximum_select_fusion.1.cells, f32[1,384]{1,0:T(1,128)S(1)} %reshape.13.gain, bf16[3,3456,384]{2,1,0:T(8,128)(2,1)S(1)} %bitcast.3), custom_call_target="tpu_custom_call" | custom-call | flops 5000000000 | bytes 1048576 | tf_op jit(solution)/shard_map/pallas_call | solution.py:189
  22.5 9.4 %collective-permute-done.2 = bf16[2,4,64,384]{3,2,1,0:T(8,128)(2,1)S(1)} collective-permute-done((bf16[2,4,64,384]{3,2,1,0:T(8,128)(2,1)S(1)}, bf16[2,4,64,384]{3,2,1,0:T(8,128)(2,1)S(1)}, u32[]{:S(2)}, u32[]{:S(2)}) %collective-permute-start.2) | collective-permute-done | bytes 393248 | tf_op jit(solution)/shard_map/ppermute | solution.py:40
  32.0 4.3 %collective-permute-start.5 = (bf16[2,4,64,384]{3,2,1,0:T(8,128)(2,1)S(1)}, bf16[2,4,64,384]{3,2,1,0:T(8,128)(2,1)S(1)}, u32[]{:S(2)}, u32[]{:S(2)}) collective-permute-start(bf16[2,4,64,384]{3,2,1,0:T(8,128)(2,1)S(1)} %collective-permute-done.2), channel_id=1, source_target_pairs={{48,32},{49,33},{50,34},{51,35},{52,36},{53,37},{54,38},{55,39},{5... | collective-permute-start | bytes 1179656 | tf_op jit(solution)/shard_map/ppermute | solution.py:40
  36.3 0.0 collective-permute-done.1.cells
  36.3 5.4 %collective-permute-start.6 = (bf16[2,4,40,384]{3,2,1,0:T(8,128)(2,1)S(1)}, bf16[2,4,40,384]{3,2,1,0:T(8,128)(2,1)S(1)}, u32[]{:S(2)}, u32[]{:S(2)}) collective-permute-start(bf16[2,4,40,384]{3,2,1,0:T(8,128)(2,1)S(1)} %slice.7), channel_id=1, source_target_pairs={{0,16},{1,17},{2,18},{3,19},{4,20},{5,21},{6,22},{7,23},{8,24},{9,... | collective-permute-start | bytes 737288 | tf_op jit(solution)/shard_map/ppermute | solution.py:40
  41.7 0.1 fusion
  41.8 7.2 %collective-permute-start.3 = (bf16[4,1,104,384]{3,2,1,0:T(8,128)(2,1)S(1)}, bf16[4,1,104,384]{3,2,1,0:T(8,128)(2,1)S(1)}, u32[]{:S(2)}, u32[]{:S(2)}) collective-permute-start(bf16[4,1,104,384]{3,2,1,0:T(8,128)(2,1)S(1)} %get-tuple-element.32), channel_id=1, source_target_pairs={{1,8},{2,9},{3,10},{4,11},{5,12},{6,13},{7,14},{8,1},{9,2},{10,3},... | collective-permute-start | bytes 958472 | tf_op jit(solution)/shard_map/ppermute | solution.py:40
  49.0 0.1 collective-permute-start.4
  49.1 9.5 %shard_map.47 = (f32[2,448,384]{2,1,0:T(8,128)S(1)}, f32[2,448,384]{2,1,0:T(8,128)S(1)}) custom-call(bf16[2,4,104,384]{3,2,1,0:T(8,128)(2,1)S(1)} %collective-permute-done.1.cells, f32[1,384]{1,0:T(1,128)S(1)} %reshape.13.gain, bf16[3,3456,384]{2,1,0:T(8,128)(2,1)S(1)} %get-tuple-element.22.weight, f32[2,448,384]{2,1,0:T(8,128)S(1)} %get-tuple-element.23.own), custom_call_target="tpu_custom_call" | custom-call | flops 10000000000 | bytes 1048576 | tf_op jit(solution)/shard_map/pallas_call | solution.py:189
  58.6 0.0 collective-permute-done.5.away
  58.6 0.0 collective-permute-done.6.near
  58.7 0.6 collective-permute-start.8
  59.3 0.0 copy-start.1
  59.4 3.4 %collective-permute-start.7 = (bf16[2,1,104,384]{3,2,1,0:T(8,128)(2,1)S(1)}, bf16[2,1,104,384]{3,2,1,0:T(8,128)(2,1)S(1)}, u32[]{:S(2)}, u32[]{:S(2)}) collective-permute-start(bf16[2,1,104,384]{3,2,1,0:T(8,128)(2,1)S(1)} %pad_maximum_fusion), channel_id=1, source_target_pairs={{1,8},{2,9},{3,10},{4,11},{5,12},{6,13},{7,14},{8,1},{9,2},{10,3},... | collective-permute-start | bytes 479240 | tf_op jit(solution)/shard_map/ppermute | solution.py:40
  62.8 5.4 %shard_map.48.middle = f32[2,448,384]{2,1,0:T(8,128)S(1)} custom-call(bf16[2,4,64,384]{3,2,1,0:T(8,128)(2,1)S(1)} %collective-permute-done.5.away, bf16[2,4,40,384]{3,2,1,0:T(8,128)(2,1)S(1)} %collective-permute-done.6.near, f32[1,384]{1,0:T(1,128)S(1)} %reshape.13.gain, bf16[3,3456,384]{2,1,0:T(8,128)(2,1)S(1)} %get-tuple-element.22.weight, ...), custom_call_target="tpu_custom_call" | custom-call | flops 5000000000 | bytes 1048576 | tf_op jit(solution)/shard_map/pallas_call | solution.py:189
  68.2 0.0 collective-permute-done.3.outer
  68.2 0.0 collective-permute-done.4.inner
  68.2 0.0 collective-permute-done.8.inner_old
  68.2 0.0 collective-permute-done.7.outer_old
  68.2 0.0 copy-done.1
  68.2 6.2 %shard_map.49 = (bf16[2,4,104,384]{3,2,1,0:T(8,128)(2,1)S(1)}, bf16[2,4,104,384]{3,2,1,0:T(8,128)(2,1)S(1)}) custom-call(s32[1]{0:T(128)} %bitcast.core, bf16[4,1,104,384]{3,2,1,0:T(8,128)(2,1)S(1)} %collective-permute-done.3.outer, bf16[4,1,104,384]{3,2,1,0:T(8,128)(2,1)S(1)} %collective-permute-done.4.inner, ...), custom_call_target="tpu_custom_call" | custom-call | flops 5000000000 | bytes 1048576 | tf_op jit(solution)/shard_map/pallas_call | solution.py:189
  74.4 1.2 %collective-permute-start.9 = (bf16[2,4,104,384]{3,2,1,0:T(8,128)(2,1)S(1)}, bf16[2,4,104,384]{3,2,1,0:T(8,128)(2,1)S(1)}, u32[]{:S(2)}, u32[]{:S(2)}) collective-permute-start(bf16[2,4,104,384]{3,2,1,0:T(8,128)(2,1)S(1)} %get-tuple-element.30), channel_id=1, source_target_pairs={{0,8},{1,9},{2,10},{3,11},{4,12},{5,13},{6,14},{7,15},{8,0},{9,1},... | collective-permute-start | bytes 1916936 | tf_op jit(solution)/shard_map/ppermute | solution.py:40
  75.6 1.7 %collective-permute-done.9 = bf16[2,4,104,384]{3,2,1,0:T(8,128)(2,1)S(1)} collective-permute-done((bf16[2,4,104,384]{3,2,1,0:T(8,128)(2,1)S(1)}, bf16[2,4,104,384]{3,2,1,0:T(8,128)(2,1)S(1)}, u32[]{:S(2)}, u32[]{:S(2)}) %collective-permute-start.9) | collective-permute-done | bytes 639008 | tf_op jit(solution)/shard_map/ppermute | solution.py:40
  77.3 1.3 %maximum_select_fusion = bf16[2,8,104,384]{3,2,1,0:T(8,128)(2,1)} fusion(bf16[2,4,104,384]{3,2,1,0:T(8,128)(2,1)S(1)} %collective-permute-done.9, bf16[2,4,104,384]{3,2,1,0:T(8,128)(2,1)S(1)} %get-tuple-element.29, pred[]{:T(512)S(6)} %eq.6), kind=kLoop, calls=%fused_computation.4 | loop fusion | flops 1916928 | bytes 2555905 | tf_op jit(solution)/shard_map/jit(_where)/select_n | solution.py:266
  (7 shorter events, 0.2 us)
Async XLA Ops:
  0.0 8.2 %copy-start.2 = (f32[384]{0:T(512)S(1)}, f32[384]{0:T(512)}, u32[]{:S(2)}) copy-start(f32[384]{0:T(512)} %param.5) | copy-start | bytes 4612
  1.1 2.0 %collective-permute-start = (bf16[1,4,104,384]{3,2,1,0:T(8,128)(2,1)S(1)}, bf16[1,4,104,384]{3,2,1,0:T(8,128)(2,1)S(1)}, u32[]{:S(2)}, u32[]{:S(2)}) collective-permute-start(bf16[1,4,104,384]{3,2,1,0:T(8,128)(2,1)S(1)} %get-tuple-element.34), channel_id=1, source_target_pairs={{0,8},{1,9},{2,10},{3,11},{4,12},{5,13},{6,14},{7,15},{8,0},{9,1},... | collective-permute-start | bytes 958472 | tf_op jit(solution)/shard_map/ppermute | solution.py:40
  3.3 33.0 %collective-permute-start.1 = (bf16[2,4,104,384]{3,2,1,0:T(8,128)(2,1)S(1)}, bf16[2,4,104,384]{3,2,1,0:T(8,128)(2,1)S(1)}, u32[]{:S(2)}, u32[]{:S(2)}) collective-permute-start(bf16[2,4,104,384]{3,2,1,0:T(8,128)(2,1)S(1)} %maximum_select_fusion.1.cells), channel_id=1, source_target_pairs={{0,16},{1,17},{2,18},{3,19},{4,20},{5,21},{6,22},{7,23},{8,24},{9,... | collective-permute-start | bytes 1916936 | tf_op jit(solution)/shard_map/ppermute | solution.py:40
  8.3 23.7 %collective-permute-start.2 = (bf16[2,4,64,384]{3,2,1,0:T(8,128)(2,1)S(1)}, bf16[2,4,64,384]{3,2,1,0:T(8,128)(2,1)S(1)}, u32[]{:S(2)}, u32[]{:S(2)}) collective-permute-start(bf16[2,4,64,384]{3,2,1,0:T(8,128)(2,1)S(1)} %slice.8), channel_id=1, source_target_pairs={{0,48},{1,49},{2,50},{3,51},{4,52},{5,53},{6,54},{7,55},{8,56},{9,... | collective-permute-start | bytes 1179656 | tf_op jit(solution)/shard_map/ppermute | solution.py:40
  13.2 3.3 %copy-start = (bf16[3,3,3,384,384]{4,3,2,1,0:T(8,128)(2,1)S(1)}, bf16[3,3,3,384,384]{4,3,2,1,0:T(8,128)(2,1)}, u32[]{:S(2)}) copy-start(bf16[3,3,3,384,384]{4,3,2,1,0:T(8,128)(2,1)} %param.6) | copy-start | bytes 23887876
  32.0 26.7 %collective-permute-start.5 = (bf16[2,4,64,384]{3,2,1,0:T(8,128)(2,1)S(1)}, bf16[2,4,64,384]{3,2,1,0:T(8,128)(2,1)S(1)}, u32[]{:S(2)}, u32[]{:S(2)}) collective-permute-start(bf16[2,4,64,384]{3,2,1,0:T(8,128)(2,1)S(1)} %collective-permute-done.2), channel_id=1, source_target_pairs={{48,32},{49,33},{50,34},{51,35},{52,36},{53,37},{54,38},{55,39},{5... | collective-permute-start | bytes 1179656 | tf_op jit(solution)/shard_map/ppermute | solution.py:40
  36.3 22.3 %collective-permute-start.6 = (bf16[2,4,40,384]{3,2,1,0:T(8,128)(2,1)S(1)}, bf16[2,4,40,384]{3,2,1,0:T(8,128)(2,1)S(1)}, u32[]{:S(2)}, u32[]{:S(2)}) collective-permute-start(bf16[2,4,40,384]{3,2,1,0:T(8,128)(2,1)S(1)} %slice.7), channel_id=1, source_target_pairs={{0,16},{1,17},{2,18},{3,19},{4,20},{5,21},{6,22},{7,23},{8,24},{9,... | collective-permute-start | bytes 737288 | tf_op jit(solution)/shard_map/ppermute | solution.py:40
  41.8 26.4 %collective-permute-start.3 = (bf16[4,1,104,384]{3,2,1,0:T(8,128)(2,1)S(1)}, bf16[4,1,104,384]{3,2,1,0:T(8,128)(2,1)S(1)}, u32[]{:S(2)}, u32[]{:S(2)}) collective-permute-start(bf16[4,1,104,384]{3,2,1,0:T(8,128)(2,1)S(1)} %get-tuple-element.32), channel_id=1, source_target_pairs={{1,8},{2,9},{3,10},{4,11},{5,12},{6,13},{7,14},{8,1},{9,2},{10,3},... | collective-permute-start | bytes 958472 | tf_op jit(solution)/shard_map/ppermute | solution.py:40
  49.0 19.2 %collective-permute-start.4 = (bf16[4,1,104,384]{3,2,1,0:T(8,128)(2,1)S(1)}, bf16[4,1,104,384]{3,2,1,0:T(8,128)(2,1)S(1)}, u32[]{:S(2)}, u32[]{:S(2)}) collective-permute-start(bf16[4,1,104,384]{3,2,1,0:T(8,128)(2,1)S(1)} %get-tuple-element.31), channel_id=1, source_target_pairs={{0,8},{1,9},{2,10},{3,11},{4,12},{5,13},{6,14},{7,15},{8,0},{9,1},... | collective-permute-start | bytes 958472 | tf_op jit(solution)/shard_map/ppermute | solution.py:40
  58.7 9.5 %collective-permute-start.8 = (bf16[2,1,104,384]{3,2,1,0:T(8,128)(2,1)S(1)}, bf16[2,1,104,384]{3,2,1,0:T(8,128)(2,1)S(1)}, u32[]{:S(2)}, u32[]{:S(2)}) collective-permute-start(bf16[2,1,104,384]{3,2,1,0:T(8,128)(2,1)S(1)} %pad_maximum_fusion.1), channel_id=1, source_target_pairs={{0,8},{1,9},{2,10},{3,11},{4,12},{5,13},{6,14},{7,15},{8,0},{9,1},... | collective-permute-start | bytes 479240 | tf_op jit(solution)/shard_map/ppermute | solution.py:40
  59.3 8.9 %copy-start.1 = (bf16[3,384,768]{2,1,0:T(8,128)(2,1)S(1)}, bf16[3,384,768]{2,1,0:T(8,128)(2,1)}, u32[]{:S(2)}) copy-start(bf16[3,384,768]{2,1,0:T(8,128)(2,1)} %param.7) | copy-start | bytes 5308420
  59.4 8.8 %collective-permute-start.7 = (bf16[2,1,104,384]{3,2,1,0:T(8,128)(2,1)S(1)}, bf16[2,1,104,384]{3,2,1,0:T(8,128)(2,1)S(1)}, u32[]{:S(2)}, u32[]{:S(2)}) collective-permute-start(bf16[2,1,104,384]{3,2,1,0:T(8,128)(2,1)S(1)} %pad_maximum_fusion), channel_id=1, source_target_pairs={{1,8},{2,9},{3,10},{4,11},{5,12},{6,13},{7,14},{8,1},{9,2},{10,3},... | collective-permute-start | bytes 479240 | tf_op jit(solution)/shard_map/ppermute | solution.py:40
  74.4 2.9 %collective-permute-start.9 = (bf16[2,4,104,384]{3,2,1,0:T(8,128)(2,1)S(1)}, bf16[2,4,104,384]{3,2,1,0:T(8,128)(2,1)S(1)}, u32[]{:S(2)}, u32[]{:S(2)}) collective-permute-start(bf16[2,4,104,384]{3,2,1,0:T(8,128)(2,1)S(1)} %get-tuple-element.30), channel_id=1, source_target_pairs={{0,8},{1,9},{2,10},{3,11},{4,12},{5,13},{6,14},{7,15},{8,0},{9,1},... | collective-permute-start | bytes 1916936 | tf_op jit(solution)/shard_map/ppermute | solution.py:40

commit v4 on v3

v4 whole, which is shorter than its diff:
```python
import functools

import jax
import jax.numpy as jnp
from jax import lax
from jax.experimental import pallas as pl
from jax.experimental.pallas import tpu as pltpu
from jax.sharding import PartitionSpec as P

EPS = 1e-06
AXES = ("tm", "rows")
PAIRS = 16
BLOCKS = 8
PITCH = 112
CUT = 16


def device(pair, core, block):
    return (pair * 2 + core) * BLOCKS + block


def routes():
    every = [(m, c, r) for m in range(PAIRS) for c in range(2) for r in range(BLOCKS)]
    swap = [(device(m, c, r), device(m, 1 - c, r)) for m, c, r in every]
    near = [(m, c, r) for m, c, r in every if m + 1 < PAIRS]
    ahead = [(device(m, c, r), device(m + 1, c, r)) for m, c, r in near]
    crossed = [(device(m, c, r), device(m + 1, 1 - c, r)) for m, c, r in near]

    def back(m):
        return m // 4 * 4 + (m - 1) % 4

    far = [(m, c, r) for m, c, r in every if m + 2 < PAIRS]
    behind = [(device(m, c, r), device(back(m), c, r)) for m, c, r in far]
    behind_again = [(device(back(m), c, r), device(m + 2, c, r)) for m, c, r in far]
    edges = []
    for m, c, r in every:
        to = r + (1 if c else -1)
        if 0 <= to < BLOCKS:
            edges.append((device(m, c, r), device(m, 1 - c, to)))
    return swap, ahead, crossed, behind, behind_again, edges


def send(block, route):
    return lax.ppermute(block, AXES, route)


def dot(lhs, rhs):
    return jnp.dot(lhs, rhs, preferred_element_type=jnp.float32)


def columns_of(values, gain):
    values = values.astype(jnp.float32)
    scaled = values * lax.rsqrt(jnp.mean(values * values, axis=-1, keepdims=True) + EPS) * gain
    active = scaled / (1.0 + jnp.exp(-scaled))
    extra = jnp.zeros((PITCH - values.shape[0], values.shape[1]), jnp.float32)
    active = jnp.concatenate([active, extra], 0)
    shifts = (pltpu.roll(active, 1, 0), active, pltpu.roll(active, PITCH - 1, 0))
    return [shift.astype(jnp.bfloat16) for shift in shifts]


def fill_taps(row, gain, taps):
    rows, channels = taps.shape[0], taps.shape[2] // 9
    scale = gain[...]
    empty = [jnp.zeros((PITCH, channels), jnp.bfloat16)] * 3
    for q in range(rows + 2):
        columns = columns_of(row(q - 1), scale) if 0 < q <= rows else empty
        for b in range(3):
            i = q - b
            if 0 <= i < rows:
                for k in range(3):
                    start = (b * 3 + k) * channels
                    taps[i, :, start : start + channels] = columns[k]


def product(taps, weight, *times):
    lhs = taps[...].reshape(-1, taps.shape[-1])
    return dot(lhs, jnp.concatenate([weight[a] for a in times], 1))


def stage_own(core, same, cross, gain, source, total, weight, taps, done):
    rows, width, channels = same.shape[1:]
    copy = pltpu.make_async_copy(source, weight, done)
    copy.start()

    def row(f, i):
        return jnp.where(core[0] == f, same[0, i], cross[0, i])

    def fill(f, _):
        fill_taps(functools.partial(row, f), gain, taps.at[f])
        return 0

    lax.fori_loop(0, 2, fill, 0)
    total[0] = jnp.zeros(total.shape[1:], jnp.float32)
    total[1] = jnp.zeros(total.shape[1:], jnp.float32)
    copy.wait()
    older = product(taps.at[0], weight, 1, 2)
    total[2] = older[:, channels:]
    total[3] = older[:, :channels] + product(taps.at[1], weight, 2)
    for f in range(2):
        for i in range(rows):
            total[2 + f, i * PITCH : i * PITCH + width] += row(f, i).astype(jnp.float32)


def stage_frame(crossing, core, cells, gain, weight, before, total, taps):
    rows, width, channels = cells.shape[1:]
    frame = 3 - core[0] if crossing else 2 + core[0]
    fill_taps(lambda i: cells[0, i], gain, taps)
    terms = product(taps, weight, 0, 1, 2)
    rest = jnp.where(frame == 3, 0, 3)
    total[rest] = before[rest]
    for a in range(3):
        total[frame - a] = before[frame - a] + terms[:, a * channels : (a + 1) * channels]
    for i in range(rows):
        area = pl.ds(i * PITCH, width)
        total[frame - 2, area] += cells[0, i].astype(jnp.float32)


def stage_old(core, away, near, gain, weight, before, total, taps):
    rows, width, channels = away.shape[1], near.shape[2] + CUT, away.shape[3]

    def row(f, i):
        start = away[0, i, :CUT].astype(jnp.float32)
        same = jnp.concatenate([start, near[0, i].astype(jnp.float32)], 0)
        return jnp.where(core[0] == f, same, away[0, i, CUT:].astype(jnp.float32))

    def fill(f, _):
        fill_taps(functools.partial(row, f), gain, taps.at[f])
        return 0

    lax.fori_loop(0, 2, fill, 0)
    newer = product(taps.at[1], weight, 0, 1)
    total[1] = before[1] + newer[:, :channels]
    total[0] = before[0] + newer[:, channels:] + product(taps.at[0], weight, 0)
    total[2] = before[2]
    total[3] = before[3]


def stage_last(
    core, outer, inner, outer_old, inner_old, gain, weight, up, sums, keep, give, edge, lines
):
    rows, width, channels = keep.shape[1:]
    scale = gain[...]
    first = core[0] == 0
    depth = 3 * channels

    def put(j, i, value):
        value = value.astype(jnp.bfloat16)
        for o in range(2):
            if 0 <= j - o < 3:
                start = (j - o) * channels
                lines[o, i * PITCH : (i + 1) * PITCH, start : start + channels] = value

    def border(frame, top):
        far, close = (outer, inner), (outer_old, inner_old)
        same, cross = (
            ((close, 1), (close, 2)),
            ((far, 2), (close, 0)),
            ((far, 0), (far, 1)),
        )[frame // 2]
        zero, one = (same, cross) if frame % 2 else (cross, same)
        at_zero = zero[0][0 if top else 1][zero[1], 0]
        at_one = one[0][1 if top else 0][one[1], 0]
        return jnp.where(first, at_zero, at_one)

    for j in range(4):
        for i in range(1, rows - 1):
            put(j, i, sums[j, i * PITCH : (i + 1) * PITCH])
    for top in (True, False):
        for frame in range(6):
            columns = columns_of(border(frame, top), scale)
            for a in range(3):
                j = frame - a
                if 0 <= j < 4:
                    for k in range(3):
                        start = a * depth + k * channels
                        edge[j * PITCH : (j + 1) * PITCH, start : start + channels] = columns[k]
        b = 0 if top else 2
        part = [weight[a, b * depth : (b + 1) * depth] for a in range(3)]
        value = dot(edge[...], jnp.concatenate(part, 0))
        i = 0 if top else rows - 1
        for j in range(4):
            area = slice(j * PITCH, (j + 1) * PITCH)
            put(j, i, sums[j, i * PITCH : (i + 1) * PITCH] + value[area])

    def write(target, value):
        for k in range(2):
            for i in range(rows):
                piece = value[i * PITCH : i * PITCH + width, k * channels : (k + 1) * channels]
                target[k, i] = piece.astype(jnp.bfloat16)

    even = dot(lines[0], up[...])
    odd = dot(lines[1], up[...])

    @pl.when(first)
    def _():
        write(keep, even)
        write(give, odd)

    @pl.when(jnp.logical_not(first))
    def _():
        write(keep, odd)
        write(give, even)


VMEM = pl.BlockSpec(memory_space=pltpu.VMEM)
SMEM = pl.BlockSpec(memory_space=pltpu.SMEM)
ANY = pl.BlockSpec(memory_space=pl.ANY)


def call(body, outs, flops, args, scratch, specs=(), limit=26):
    specs = {0: SMEM, **dict(specs)}
    return pl.pallas_call(
        body,
        out_shape=outs,
        in_specs=[specs.get(n, VMEM) for n in range(len(args))],
        out_specs=[VMEM] * len(outs),
        scratch_shapes=scratch,
        compiler_params=pltpu.CompilerParams(vmem_limit_bytes=limit << 20),
        cost_estimate=pl.CostEstimate(flops=flops, bytes_accessed=1 << 20, transcendentals=0),
    )(*args)


def local(latents, norm_gain, conv_weight, up_weight):
    swap, ahead, crossed, behind, behind_again, edges = routes()
    core = lax.axis_index("tm") % 2
    rows, width, channels = latents.shape[1] // 2, latents.shape[2], latents.shape[3]
    gain = norm_gain.reshape(1, channels)
    source = conv_weight.reshape(3, 9 * channels, channels)
    up = up_weight.reshape(3 * channels, 2 * channels)
    mark = core.reshape(1).astype(jnp.int32)
    size = rows * PITCH
    taps = pltpu.VMEM((rows, PITCH, 9 * channels), jnp.bfloat16)
    pair = pltpu.VMEM((2, rows, PITCH, 9 * channels), jnp.bfloat16)
    totals = jax.ShapeDtypeStruct((4, size, channels), jnp.float32)
    half = jax.ShapeDtypeStruct((2, rows, width, channels), jnp.bfloat16)

    def borders(*frames):
        block = jnp.concatenate(frames, 0)
        outer = lax.dynamic_slice_in_dim(block, core * (rows - 1), 1, 1)
        inner = lax.dynamic_slice_in_dim(block, (1 - core) * (rows - 1), 1, 1)
        return send(outer, edges), send(inner, swap)

    kept = lax.dynamic_slice_in_dim(latents, core * rows, rows, 1)
    given = lax.dynamic_slice_in_dim(latents, (1 - core) * rows, rows, 1)
    same = send(kept, ahead)
    taken = send(given, swap)
    given, taken = lax.optimization_barrier((given, taken))
    cross = send(given, crossed)
    away = send(jnp.concatenate([kept[:, :, :CUT], taken], 2), behind)
    total, weight = call(
        stage_own,
        [totals, jax.ShapeDtypeStruct(source.shape, source.dtype)],
        5 * 10**9,
        (mark, kept, taken, gain, source),
        [pair, pltpu.SemaphoreType.DMA],
        {4: ANY},
        limit=46,
    )
    same, total = lax.optimization_barrier((same, total))
    near = send(same[:, :, CUT:], ahead)
    same, away, total = lax.optimization_barrier((same, away, total))
    away = send(away, behind_again)
    near_borders = borders(kept, taken, same)
    (total,) = call(
        functools.partial(stage_frame, False),
        [totals],
        10**9,
        (mark, same, gain, weight, total),
        [taps],
    )
    cross, total = lax.optimization_barrier((cross, total))
    (total,) = call(
        functools.partial(stage_frame, True),
        [totals],
        10**9,
        (mark, cross, gain, weight, total),
        [taps],
    )
    away, near, total = lax.optimization_barrier((away, near, total))
    old = jnp.concatenate([away[:, :, :CUT], near], 2)
    old_borders = borders(cross, old, away[:, :, CUT:])
    (total,) = call(
        stage_old, [totals], 5 * 10**9, (mark, away, near, gain, weight, total), [pair]
    )
    keep, give = call(
        stage_last,
        [half, half],
        5 * 10**9,
        (mark, *near_borders, *old_borders, gain, weight, up, total),
        [
            pltpu.VMEM((size, 9 * channels), jnp.bfloat16),
            pltpu.VMEM((2, size, 3 * channels), jnp.bfloat16),
        ],
    )
    got = send(give, swap)
    return jnp.where(
        core == 0, jnp.concatenate([keep, got], 1), jnp.concatenate([got, keep], 1)
    )


def solution(mesh):
    placed = (P("tm", "rows", None, None), P(), P(), P())
    return jax.shard_map(
        local, mesh=mesh, in_specs=placed, out_specs=P("tm", "rows", None, None), check_vma=False
    )
```

time: 78.9 us -> 79.3 us (level); the launches traced: 78.6 us -> 78.1 us
  waiting for transfers between devices: 12.4 us -> 7.69 us
  Pallas kernels: 27.1 us -> 30 us
  local copies, waits for them, and re-layouts: 4.53 us -> 6.09 us
    ppermute x10 -> x11, waiting for transfers between devices: 12.4 us -> 7.69 us  [send(): return lax.ppermute(block, AXES, route)]
    pallas_call x4 -> x5, Pallas kernels: 27.1 us -> 30 us  [call(): pl.pallas_call(body, out_shape=outs, in_specs=[specs.get(n, VMEM) for n i...]
    slice x2 -> x4, local copies, waits for them, and re-layouts: 0.07 us -> 0.87 us  [the longest x1 0.8 us: local(): away = send(jnp.concatenate([kept[:, :, :CUT], taken], 2), behind)]
    ppermute x10 -> x11, starting transfers between devices: 32.8 us -> 32.4 us  [send(): return lax.ppermute(block, AXES, route)]
  transfers between devices with their start and end apart: 10 -> 11, of which waited for: 3 -> 3; matrix products, arithmetic and copies ran while one was open for 0% -> 3% of each run, Pallas kernels for 27% -> 31%
where the time goes in v4:
time: 79.3 us; the launch traced here: 78.1 us
  starting transfers between devices  32.4 us (41%)
  Pallas kernels  30 us (38%)
  waiting for transfers between devices  7.69 us (10%)
  local copies, waits for them, and re-layouts  6.09 us (8%)
  other arithmetic  1.6 us (2%)
    ppermute x11, starting transfers between devices, send(): return lax.ppermute(block, AXES, route)  32.4 us
    pallas_call x5, Pallas kernels, call(): pl.pallas_call(body, out_shape=outs, in_specs=[specs.get(n, VMEM) for n i...  30 us
    ppermute x11, waiting for transfers between devices, send(): return lax.ppermute(block, AXES, route)  7.69 us
    unnamed x6, local copies, waits for them, and re-layouts  3.26 us
  transfers between devices with their start and end apart: 11, of which 3 were waited for; matrix products, arithmetic and copies ran while one was open for 3% of the time, Pallas kernels for 31%

profile of v4, /device:TPU:29, one launch (start us, length us, event | category | flops | bytes accessed | tf_op | source)
XLA Modules:
  0.0 78.1 jit_solution(657416591384795820)
XLA Ops:
  0.0 1.1 %constant_dynamic-slice_fusion.5 = (bf16[1,4,104,384]{3,2,1,0:T(8,128)(2,1)S(1)}, bf16[1,4,104,384]{3,2,1,0:T(8,128)(2,1)S(1)}) fusion(bf16[1,8,104,384]{3,2,1,0:T(8,128)(2,1)} %param.4, s32[]{:T(128)S(6)} %select_n.32, s32[]{:T(128)S(6)} %select_n.31), kind=kLoop, calls=%fused_computation.9 | loop fusion | bytes 1277960 | tf_op jit(solution)/shard_map/dynamic_slice | solution.py:244
  1.1 0.8 collective-permute-start
  1.9 4.9 %collective-permute-start.1 = (bf16[1,4,104,384]{3,2,1,0:T(8,128)(2,1)S(1)}, bf16[1,4,104,384]{3,2,1,0:T(8,128)(2,1)S(1)}, u32[]{:S(2)}, u32[]{:S(2)}) collective-permute-start(bf16[1,4,104,384]{3,2,1,0:T(8,128)(2,1)S(1)} %get-tuple-element.42.same), channel_id=1, source_target_pairs={{0,16},{1,17},{2,18},{3,19},{4,20},{5,21},{6,22},{7,23},{8,24},{9,... | collective-permute-start | bytes 958472 | tf_op jit(solution)/shard_map/ppermute | solution.py:44
  6.8 0.7 reshape.13.gain
  7.5 0.8 %constant_dynamic-slice_fusion = bf16[1,4,16,384]{3,2,1,0:T(8,128)(2,1)S(1)} fusion(bf16[1,8,104,384]{3,2,1,0:T(8,128)(2,1)} %param.4, s32[]{:T(128)S(6)} %select_n.31), kind=kLoop, calls=%fused_computation.4 | loop fusion | bytes 98308 | tf_op jit(solution)/shard_map/slice | solution.py:249
  8.3 0.0 collective-permute-done.cross
  8.3 6.3 %collective-permute-start.5 = (bf16[1,4,104,384]{3,2,1,0:T(8,128)(2,1)S(1)}, bf16[1,4,104,384]{3,2,1,0:T(8,128)(2,1)S(1)}, u32[]{:S(2)}, u32[]{:S(2)}) collective-permute-start(bf16[1,4,104,384]{3,2,1,0:T(8,128)(2,1)S(1)} %get-tuple-element.26), channel_id=1, source_target_pairs={{0,24},{1,25},{2,26},{3,27},{4,28},{5,29},{6,30},{7,31},{8,16},{9,... | collective-permute-start | bytes 958472 | tf_op jit(solution)/shard_map/ppermute | solution.py:44
  14.6 1.9 %collective-permute-start.2 = (bf16[1,4,120,384]{3,2,1,0:T(8,128)(2,1)S(1)}, bf16[1,4,120,384]{3,2,1,0:T(8,128)(2,1)S(1)}, u32[]{:S(2)}, u32[]{:S(2)}) collective-permute-start(bf16[1,4,120,384]{3,2,1,0:T(8,128)(2,1)S(1)} %pad_maximum_fusion.2), channel_id=1, source_target_pairs={{0,48},{1,49},{2,50},{3,51},{4,52},{5,53},{6,54},{7,55},{8,56},{9,... | collective-permute-start | bytes 1105928 | tf_op jit(solution)/shard_map/ppermute | solution.py:44
  16.6 8.9 %shard_map.46 = (f32[4,448,384]{2,1,0:T(8,128)S(1)}, bf16[3,3456,384]{2,1,0:T(8,128)(2,1)}) custom-call(s32[1]{0:T(128)} %bitcast.core, bf16[1,4,104,384]{3,2,1,0:T(8,128)(2,1)S(1)} %get-tuple-element.42.same, bf16[1,4,104,384]{3,2,1,0:T(8,128)(2,1)S(1)} %collective-permute-done.cross, f32[1,384]{1,0:T(1,128)S(1)} %reshape.13.gain, bf16[3,3456,384]{2,1,0:T(8,128)(2,1)} %bitcast.4), custom_call_target="tpu_custom_call" | custom-call | flops 5000000000 | bytes 1048576 | tf_op jit(solution)/shard_map/pallas_call | solution.py:212
  25.5 0.0 collective-permute-done.1.cells
  25.6 4.3 %collective-permute-start.7 = (bf16[1,4,88,384]{3,2,1,0:T(8,128)(2,1)S(1)}, bf16[1,4,88,384]{3,2,1,0:T(8,128)(2,1)S(1)}, u32[]{:S(2)}, u32[]{:S(2)}) collective-permute-start(bf16[1,4,88,384]{3,2,1,0:T(8,128)(2,1)S(1)} %slice.13), channel_id=1, source_target_pairs={{0,16},{1,17},{2,18},{3,19},{4,20},{5,21},{6,22},{7,23},{8,24},{9,... | collective-permute-start | bytes 811016 | tf_op jit(solution)/shard_map/ppermute | solution.py:44
  29.8 5.6 %collective-permute-done.2 = bf16[1,4,120,384]{3,2,1,0:T(8,128)(2,1)S(1)} collective-permute-done((bf16[1,4,120,384]{3,2,1,0:T(8,128)(2,1)S(1)}, bf16[1,4,120,384]{3,2,1,0:T(8,128)(2,1)S(1)}, u32[]{:S(2)}, u32[]{:S(2)}) %collective-permute-start.2) | collective-permute-done | bytes 368672 | tf_op jit(solution)/shard_map/ppermute | solution.py:44
  35.4 3.0 %collective-permute-start.6 = (bf16[1,4,120,384]{3,2,1,0:T(8,128)(2,1)S(1)}, bf16[1,4,120,384]{3,2,1,0:T(8,128)(2,1)S(1)}, u32[]{:S(2)}, u32[]{:S(2)}) collective-permute-start(bf16[1,4,120,384]{3,2,1,0:T(8,128)(2,1)S(1)} %collective-permute-done.2), channel_id=1, source_target_pairs={{48,32},{49,33},{50,34},{51,35},{52,36},{53,37},{54,38},{55,39},{5... | collective-permute-start | bytes 1105928 | tf_op jit(solution)/shard_map/ppermute | solution.py:44
  38.5 0.1 pad_maximum_fusion
  38.6 0.0 copy-start
  38.6 3.3 %copy-done = bf16[3,3456,384]{2,1,0:T(8,128)(2,1)S(1)} copy-done((bf16[3,3456,384]{2,1,0:T(8,128)(2,1)S(1)}, bf16[3,3456,384]{2,1,0:T(8,128)(2,1)}, u32[]{:S(2)}) %copy-start) | copy-done | bytes 7962648
  41.9 0.0 copy-start.1
  41.9 4.7 %shard_map.47.before = f32[4,448,384]{2,1,0:T(8,128)S(1)} custom-call(s32[1]{0:T(128)} %bitcast.core, bf16[1,4,104,384]{3,2,1,0:T(8,128)(2,1)S(1)} %collective-permute-done.1.cells, f32[1,384]{1,0:T(1,128)S(1)} %reshape.13.gain, bf16[3,3456,384]{2,1,0:T(8,128)(2,1)S(1)} %copy-done, f32[4,448,384]{2,1,0:T(8,128)S(1)} %get-tuple-element.28.before), custom_call_target="tpu_custom_call" | custom-call | flops 1000000000 | bytes 1048576 | tf_op jit(solution)/shard_map/pallas_call | solution.py:212
  46.6 0.0 collective-permute-done.5.cells
  46.6 0.1 constant_dynamic-slice_fusion.3
  46.7 1.4 %collective-permute-start.4 = (bf16[3,1,104,384]{3,2,1,0:T(8,128)(2,1)S(1)}, bf16[3,1,104,384]{3,2,1,0:T(8,128)(2,1)S(1)}, u32[]{:S(2)}, u32[]{:S(2)}) collective-permute-start(bf16[3,1,104,384]{3,2,1,0:T(8,128)(2,1)S(1)} %get-tuple-element.39), channel_id=1, source_target_pairs={{0,8},{1,9},{2,10},{3,11},{4,12},{5,13},{6,14},{7,15},{8,0},{9,1},... | collective-permute-start | bytes 718856 | tf_op jit(solution)/shard_map/ppermute | solution.py:44
  48.1 4.1 %collective-permute-start.3 = (bf16[3,1,104,384]{3,2,1,0:T(8,128)(2,1)S(1)}, bf16[3,1,104,384]{3,2,1,0:T(8,128)(2,1)S(1)}, u32[]{:S(2)}, u32[]{:S(2)}) collective-permute-start(bf16[3,1,104,384]{3,2,1,0:T(8,128)(2,1)S(1)} %get-tuple-element.40), channel_id=1, source_target_pairs={{1,8},{2,9},{3,10},{4,11},{5,12},{6,13},{7,14},{8,1},{9,2},{10,3},... | collective-permute-start | bytes 718856 | tf_op jit(solution)/shard_map/ppermute | solution.py:44
  52.1 0.0 copy-done.1
  52.1 4.8 %shard_map.48.before = f32[4,448,384]{2,1,0:T(8,128)S(1)} custom-call(s32[1]{0:T(128)} %bitcast.core, bf16[1,4,104,384]{3,2,1,0:T(8,128)(2,1)S(1)} %collective-permute-done.5.cells, f32[1,384]{1,0:T(1,128)S(1)} %reshape.13.gain, bf16[3,3456,384]{2,1,0:T(8,128)(2,1)S(1)} %copy-done.1, f32[4,448,384]{2,1,0:T(8,128)S(1)} %shard_map.47.before), custom_call_target="tpu_custom_call" | custom-call | flops 1000000000 | bytes 1048576 | tf_op jit(solution)/shard_map/pallas_call | solution.py:212
  57.0 0.0 collective-permute-done.7.near
  57.0 0.0 collective-permute-done.6.away
  57.0 0.1 pad_maximum_fusion.1
  57.1 0.1 constant_dynamic-slice_fusion.1
  57.2 0.9 %collective-permute-start.9 = (bf16[3,1,104,384]{3,2,1,0:T(8,128)(2,1)S(1)}, bf16[3,1,104,384]{3,2,1,0:T(8,128)(2,1)S(1)}, u32[]{:S(2)}, u32[]{:S(2)}) collective-permute-start(bf16[3,1,104,384]{3,2,1,0:T(8,128)(2,1)S(1)} %get-tuple-element.37), channel_id=1, source_target_pairs={{0,8},{1,9},{2,10},{3,11},{4,12},{5,13},{6,14},{7,15},{8,0},{9,1},... | collective-permute-start | bytes 718856 | tf_op jit(solution)/shard_map/ppermute | solution.py:44
  58.1 0.0 copy-start.2
  58.1 2.0 %collective-permute-start.8 = (bf16[3,1,104,384]{3,2,1,0:T(8,128)(2,1)S(1)}, bf16[3,1,104,384]{3,2,1,0:T(8,128)(2,1)S(1)}, u32[]{:S(2)}, u32[]{:S(2)}) collective-permute-start(bf16[3,1,104,384]{3,2,1,0:T(8,128)(2,1)S(1)} %get-tuple-element.38), channel_id=1, source_target_pairs={{1,8},{2,9},{3,10},{4,11},{5,12},{6,13},{7,14},{8,1},{9,2},{10,3},... | collective-permute-start | bytes 718856 | tf_op jit(solution)/shard_map/ppermute | solution.py:44
  60.1 5.4 %shard_map.49.sums = f32[4,448,384]{2,1,0:T(8,128)S(1)} custom-call(s32[1]{0:T(128)} %bitcast.core, bf16[1,4,120,384]{3,2,1,0:T(8,128)(2,1)S(1)} %collective-permute-done.6.away, bf16[1,4,88,384]{3,2,1,0:T(8,128)(2,1)S(1)} %collective-permute-done.7.near, f32[1,384]{1,0:T(1,128)S(1)} %reshape.13.gain, bf16[3,3456,384]{2,1,0:T(8,128)(2,1)S(1)} %copy-done.1, ...), custom_call_target="tpu_custom_call" | custom-call | flops 5000000000 | bytes 1048576 | tf_op jit(solution)/shard_map/pallas_call | solution.py:212
  65.6 0.0 collective-permute-done.4.inner
  65.6 0.0 collective-permute-done.3.outer
  65.6 0.0 collective-permute-done.9.inner_old
  65.6 0.4 collective-permute-done.8.outer_old
  66.0 0.0 copy-done.2
  66.0 6.2 %shard_map.50 = (bf16[2,4,104,384]{3,2,1,0:T(8,128)(2,1)S(1)}, bf16[2,4,104,384]{3,2,1,0:T(8,128)(2,1)S(1)}) custom-call(s32[1]{0:T(128)} %bitcast.core, bf16[3,1,104,384]{3,2,1,0:T(8,128)(2,1)S(1)} %collective-permute-done.3.outer, bf16[3,1,104,384]{3,2,1,0:T(8,128)(2,1)S(1)} %collective-permute-done.4.inner, ...), custom_call_target="tpu_custom_call" | custom-call | flops 5000000000 | bytes 1048576 | tf_op jit(solution)/shard_map/pallas_call | solution.py:212
  72.1 2.9 %collective-permute-start.10 = (bf16[2,4,104,384]{3,2,1,0:T(8,128)(2,1)S(1)}, bf16[2,4,104,384]{3,2,1,0:T(8,128)(2,1)S(1)}, u32[]{:S(2)}, u32[]{:S(2)}) collective-permute-start(bf16[2,4,104,384]{3,2,1,0:T(8,128)(2,1)S(1)} %get-tuple-element.36), channel_id=1, source_target_pairs={{0,8},{1,9},{2,10},{3,11},{4,12},{5,13},{6,14},{7,15},{8,0},{9,1},... | collective-permute-start | bytes 1916936 | tf_op jit(solution)/shard_map/ppermute | solution.py:44
  75.0 1.7 %collective-permute-done.10 = bf16[2,4,104,384]{3,2,1,0:T(8,128)(2,1)S(1)} collective-permute-done((bf16[2,4,104,384]{3,2,1,0:T(8,128)(2,1)S(1)}, bf16[2,4,104,384]{3,2,1,0:T(8,128)(2,1)S(1)}, u32[]{:S(2)}, u32[]{:S(2)}) %collective-permute-start.10) | collective-permute-done | bytes 639008 | tf_op jit(solution)/shard_map/ppermute | solution.py:44
  76.7 1.3 %maximum_select_fusion = bf16[2,8,104,384]{3,2,1,0:T(8,128)(2,1)} fusion(bf16[2,4,104,384]{3,2,1,0:T(8,128)(2,1)S(1)} %collective-permute-done.10, bf16[2,4,104,384]{3,2,1,0:T(8,128)(2,1)S(1)} %get-tuple-element.35, pred[]{:T(512)S(6)} %eq.5), kind=kLoop, calls=%fused_computation | loop fusion | flops 1916928 | bytes 2555905 | tf_op jit(solution)/shard_map/jit(_where)/select_n | solution.py:296
  (4 shorter events, 0.1 us)
Async XLA Ops:
  1.1 7.2 %collective-permute-start = (bf16[1,4,104,384]{3,2,1,0:T(8,128)(2,1)S(1)}, bf16[1,4,104,384]{3,2,1,0:T(8,128)(2,1)S(1)}, u32[]{:S(2)}, u32[]{:S(2)}) collective-permute-start(bf16[1,4,104,384]{3,2,1,0:T(8,128)(2,1)S(1)} %get-tuple-element.26), channel_id=1, source_target_pairs={{0,8},{1,9},{2,10},{3,11},{4,12},{5,13},{6,14},{7,15},{8,0},{9,1},... | collective-permute-start | bytes 958472 | tf_op jit(solution)/shard_map/ppermute | solution.py:44
  1.9 23.6 %collective-permute-start.1 = (bf16[1,4,104,384]{3,2,1,0:T(8,128)(2,1)S(1)}, bf16[1,4,104,384]{3,2,1,0:T(8,128)(2,1)S(1)}, u32[]{:S(2)}, u32[]{:S(2)}) collective-permute-start(bf16[1,4,104,384]{3,2,1,0:T(8,128)(2,1)S(1)} %get-tuple-element.42.same), channel_id=1, source_target_pairs={{0,16},{1,17},{2,18},{3,19},{4,20},{5,21},{6,22},{7,23},{8,24},{9,... | collective-permute-start | bytes 958472 | tf_op jit(solution)/shard_map/ppermute | solution.py:44
  8.3 38.3 %collective-permute-start.5 = (bf16[1,4,104,384]{3,2,1,0:T(8,128)(2,1)S(1)}, bf16[1,4,104,384]{3,2,1,0:T(8,128)(2,1)S(1)}, u32[]{:S(2)}, u32[]{:S(2)}) collective-permute-start(bf16[1,4,104,384]{3,2,1,0:T(8,128)(2,1)S(1)} %get-tuple-element.26), channel_id=1, source_target_pairs={{0,24},{1,25},{2,26},{3,27},{4,28},{5,29},{6,30},{7,31},{8,16},{9,... | collective-permute-start | bytes 958472 | tf_op jit(solution)/shard_map/ppermute | solution.py:44
  14.6 20.8 %collective-permute-start.2 = (bf16[1,4,120,384]{3,2,1,0:T(8,128)(2,1)S(1)}, bf16[1,4,120,384]{3,2,1,0:T(8,128)(2,1)S(1)}, u32[]{:S(2)}, u32[]{:S(2)}) collective-permute-start(bf16[1,4,120,384]{3,2,1,0:T(8,128)(2,1)S(1)} %pad_maximum_fusion.2), channel_id=1, source_target_pairs={{0,48},{1,49},{2,50},{3,51},{4,52},{5,53},{6,54},{7,55},{8,56},{9,... | collective-permute-start | bytes 1105928 | tf_op jit(solution)/shard_map/ppermute | solution.py:44
  25.6 31.4 %collective-permute-start.7 = (bf16[1,4,88,384]{3,2,1,0:T(8,128)(2,1)S(1)}, bf16[1,4,88,384]{3,2,1,0:T(8,128)(2,1)S(1)}, u32[]{:S(2)}, u32[]{:S(2)}) collective-permute-start(bf16[1,4,88,384]{3,2,1,0:T(8,128)(2,1)S(1)} %slice.13), channel_id=1, source_target_pairs={{0,16},{1,17},{2,18},{3,19},{4,20},{5,21},{6,22},{7,23},{8,24},{9,... | collective-permute-start | bytes 811016 | tf_op jit(solution)/shard_map/ppermute | solution.py:44
  35.4 21.5 %collective-permute-start.6 = (bf16[1,4,120,384]{3,2,1,0:T(8,128)(2,1)S(1)}, bf16[1,4,120,384]{3,2,1,0:T(8,128)(2,1)S(1)}, u32[]{:S(2)}, u32[]{:S(2)}) collective-permute-start(bf16[1,4,120,384]{3,2,1,0:T(8,128)(2,1)S(1)} %collective-permute-done.2), channel_id=1, source_target_pairs={{48,32},{49,33},{50,34},{51,35},{52,36},{53,37},{54,38},{55,39},{5... | collective-permute-start | bytes 1105928 | tf_op jit(solution)/shard_map/ppermute | solution.py:44
  38.6 3.3 %copy-start = (bf16[3,3456,384]{2,1,0:T(8,128)(2,1)S(1)}, bf16[3,3456,384]{2,1,0:T(8,128)(2,1)}, u32[]{:S(2)}) copy-start(bf16[3,3456,384]{2,1,0:T(8,128)(2,1)} %get-tuple-element.27.weight) | copy-start | bytes 23887876
  41.9 10.3 %copy-start.1 = (bf16[3,3456,384]{2,1,0:T(8,128)(2,1)S(1)}, bf16[3,3456,384]{2,1,0:T(8,128)(2,1)}, u32[]{:S(2)}) copy-start(bf16[3,3456,384]{2,1,0:T(8,128)(2,1)} %get-tuple-element.27.weight) | copy-start | bytes 23887876
  46.7 18.9 %collective-permute-start.4 = (bf16[3,1,104,384]{3,2,1,0:T(8,128)(2,1)S(1)}, bf16[3,1,104,384]{3,2,1,0:T(8,128)(2,1)S(1)}, u32[]{:S(2)}, u32[]{:S(2)}) collective-permute-start(bf16[3,1,104,384]{3,2,1,0:T(8,128)(2,1)S(1)} %get-tuple-element.39), channel_id=1, source_target_pairs={{0,8},{1,9},{2,10},{3,11},{4,12},{5,13},{6,14},{7,15},{8,0},{9,1},... | collective-permute-start | bytes 718856 | tf_op jit(solution)/shard_map/ppermute | solution.py:44
  48.1 17.5 %collective-permute-start.3 = (bf16[3,1,104,384]{3,2,1,0:T(8,128)(2,1)S(1)}, bf16[3,1,104,384]{3,2,1,0:T(8,128)(2,1)S(1)}, u32[]{:S(2)}, u32[]{:S(2)}) collective-permute-start(bf16[3,1,104,384]{3,2,1,0:T(8,128)(2,1)S(1)} %get-tuple-element.40), channel_id=1, source_target_pairs={{1,8},{2,9},{3,10},{4,11},{5,12},{6,13},{7,14},{8,1},{9,2},{10,3},... | collective-permute-start | bytes 718856 | tf_op jit(solution)/shard_map/ppermute | solution.py:44
  57.2 8.4 %collective-permute-start.9 = (bf16[3,1,104,384]{3,2,1,0:T(8,128)(2,1)S(1)}, bf16[3,1,104,384]{3,2,1,0:T(8,128)(2,1)S(1)}, u32[]{:S(2)}, u32[]{:S(2)}) collective-permute-start(bf16[3,1,104,384]{3,2,1,0:T(8,128)(2,1)S(1)} %get-tuple-element.37), channel_id=1, source_target_pairs={{0,8},{1,9},{2,10},{3,11},{4,12},{5,13},{6,14},{7,15},{8,0},{9,1},... | collective-permute-start | bytes 718856 | tf_op jit(solution)/shard_map/ppermute | solution.py:44
  58.1 7.9 %copy-start.2 = (bf16[3,384,768]{2,1,0:T(8,128)(2,1)S(1)}, bf16[3,384,768]{2,1,0:T(8,128)(2,1)}, u32[]{:S(2)}) copy-start(bf16[3,384,768]{2,1,0:T(8,128)(2,1)} %param.7) | copy-start | bytes 5308420
  58.1 7.9 %collective-permute-start.8 = (bf16[3,1,104,384]{3,2,1,0:T(8,128)(2,1)S(1)}, bf16[3,1,104,384]{3,2,1,0:T(8,128)(2,1)S(1)}, u32[]{:S(2)}, u32[]{:S(2)}) collective-permute-start(bf16[3,1,104,384]{3,2,1,0:T(8,128)(2,1)S(1)} %get-tuple-element.38), channel_id=1, source_target_pairs={{1,8},{2,9},{3,10},{4,11},{5,12},{6,13},{7,14},{8,1},{9,2},{10,3},... | collective-permute-start | bytes 718856 | tf_op jit(solution)/shard_map/ppermute | solution.py:44
  72.1 4.6 %collective-permute-start.10 = (bf16[2,4,104,384]{3,2,1,0:T(8,128)(2,1)S(1)}, bf16[2,4,104,384]{3,2,1,0:T(8,128)(2,1)S(1)}, u32[]{:S(2)}, u32[]{:S(2)}) collective-permute-start(bf16[2,4,104,384]{3,2,1,0:T(8,128)(2,1)S(1)} %get-tuple-element.36), channel_id=1, source_target_pairs={{0,8},{1,9},{2,10},{3,11},{4,12},{5,13},{6,14},{7,15},{8,0},{9,1},... | collective-permute-start | bytes 1916936 | tf_op jit(solution)/shard_map/ppermute | solution.py:44

commit v5 on v3

--- a/solution.py
+++ b/solution.py
@@ -121,9 +121,9 @@
 
 
 def stage_last(
-    core, outer, inner, outer_old, inner_old, gain, weight, up, own, middle, keep, give, edge, lines
+    core, outer, inner, outer_old, inner_old, gain, weight, up, own, middle, give, lines, edge
 ):
-    rows, width, channels = keep.shape[1:]
+    rows, width, channels = give.shape[1:]
     scale = gain[...]
     first = core[0] == 0
     depth = 3 * channels
@@ -160,24 +160,19 @@
         for j in range(4):
             put(j, i, total(j, i) + value[j * PITCH : (j + 1) * PITCH])
 
-    def write(target, value):
-        for k in range(2):
-            for i in range(rows):
-                piece = value[i * PITCH : i * PITCH + width, k * channels : (k + 1) * channels]
-                target[k, i] = piece.astype(jnp.bfloat16)
-
-    even = dot(lines[0], up[...])
-    odd = dot(lines[1], up[...])
-
-    @pl.when(first)
-    def _():
-        write(keep, even)
-        write(give, odd)
-
-    @pl.when(jnp.logical_not(first))
-    def _():
-        write(keep, odd)
-        write(give, even)
+    write(give, dot(lines[1 - core[0]], up[...]))
+
+
+def write(target, value):
+    rows, width, channels = target.shape[1:]
+    for k in range(2):
+        for i in range(rows):
+            piece = value[i * PITCH : i * PITCH + width, k * channels : (k + 1) * channels]
+            target[k, i] = piece.astype(jnp.bfloat16)
+
+
+def stage_keep(core, lines, up, keep):
+    write(keep, dot(lines[core[0]], up[...]))
 
 
 VMEM = pl.BlockSpec(memory_space=pltpu.VMEM)
@@ -251,18 +246,18 @@
     (middle_total,) = call(
         stage_old, [totals], 5 * 10**9, (away, near, gain, held, middle_total), {}, [taps]
     )
-    keep, give = call(
+    give, lines = call(
         stage_last,
-        [half, half],
+        [half, jax.ShapeDtypeStruct((2, size, 3 * channels), jnp.bfloat16)],
         5 * 10**9,
         (mark, outer_near, inner_near, outer_old, inner_old, gain, held, up, own_total, middle_total),
         {0: SMEM},
         [
             pltpu.VMEM((size, 9 * channels), jnp.bfloat16),
-            pltpu.VMEM((2, size, 3 * channels), jnp.bfloat16),
         ],
     )
     got = send(give, swap)
+    (keep,) = call(stage_keep, [half], 10**9, (mark, lines, up), {0: SMEM}, [])
     return jnp.where(
         core == 0, jnp.concatenate([keep, got], 1), jnp.concatenate([got, keep], 1)
     )

time: 78.9 us -> 78.1 us (0.990)
  waiting for transfers between devices: 12.4 us -> 11.3 us
    ppermute x10, waiting for transfers between devices: 12.4 us -> 11.3 us  [send(): return lax.ppermute(block, AXES, route)]
    pallas_call x4 -> x5, Pallas kernels: 27.1 us -> 27.7 us  [call(): pl.pallas_call(body, out_shape=outs, in_specs=[specs.get(n, VMEM) for n i...]
  transfers between devices with their start and end apart: 10 -> 10, of which waited for: 3 -> 3; matrix products, arithmetic and copies ran while one was open for 0% -> 0% of each run, Pallas kernels for 27% -> 28%
where the time goes in v5:
time: 78.1 us; the launch traced here: 77.4 us
  starting transfers between devices  32.1 us (41%)
  Pallas kernels  27.7 us (35%)
  waiting for transfers between devices  11.3 us (14%)
  local copies, waits for them, and re-layouts  4.53 us (6%)
  other arithmetic  1.52 us (2%)
    ppermute x10, starting transfers between devices, send(): return lax.ppermute(block, AXES, route)  32.1 us
    pallas_call x5, Pallas kernels, call(): pl.pallas_call(body, out_shape=outs, in_specs=[specs.get(n, VMEM) for n i...  27.7 us
    ppermute x10, waiting for transfers between devices, send(): return lax.ppermute(block, AXES, route)  11.3 us
    unnamed x6, local copies, waits for them, and re-layouts  3.27 us
  transfers between devices with their start and end apart: 10, of which 3 were waited for; matrix products, arithmetic and copies ran while one was open for 0% of the time, Pallas kernels for 28%

profile of v5, /device:TPU:29, one launch (start us, length us, event | category | flops | bytes accessed | tf_op | source)
XLA Modules:
  0.0 77.4 jit_solution(4705177467773953996)
XLA Ops:
  0.0 0.0 copy-start.2
  0.0 1.1 %constant_dynamic-slice_fusion.5 = (bf16[1,4,104,384]{3,2,1,0:T(8,128)(2,1)S(1)}, bf16[1,4,104,384]{3,2,1,0:T(8,128)(2,1)S(1)}) fusion(bf16[1,8,104,384]{3,2,1,0:T(8,128)(2,1)} %param.4, s32[]{:T(128)S(6)} %select_n.42, s32[]{:T(128)S(6)} %select_n.43), kind=kLoop, calls=%fused_computation.15 | loop fusion | bytes 1277960 | tf_op jit(solution)/shard_map/dynamic_slice | solution.py:208
  1.1 0.8 collective-permute-start
  1.9 1.2 %collective-permute-done = bf16[1,4,104,384]{3,2,1,0:T(8,128)(2,1)S(1)} collective-permute-done((bf16[1,4,104,384]{3,2,1,0:T(8,128)(2,1)S(1)}, bf16[1,4,104,384]{3,2,1,0:T(8,128)(2,1)S(1)}, u32[]{:S(2)}, u32[]{:S(2)}) %collective-permute-start) | collective-permute-done | bytes 319520 | tf_op jit(solution)/shard_map/ppermute | solution.py:40
  3.2 0.1 maximum_select_fusion.1.cells
  3.3 4.9 %collective-permute-start.1 = (bf16[2,4,104,384]{3,2,1,0:T(8,128)(2,1)S(1)}, bf16[2,4,104,384]{3,2,1,0:T(8,128)(2,1)S(1)}, u32[]{:S(2)}, u32[]{:S(2)}) collective-permute-start(bf16[2,4,104,384]{3,2,1,0:T(8,128)(2,1)S(1)} %maximum_select_fusion.1.cells), channel_id=1, source_target_pairs={{0,16},{1,17},{2,18},{3,19},{4,20},{5,21},{6,22},{7,23},{8,24},{9,... | collective-permute-start | bytes 1916936 | tf_op jit(solution)/shard_map/ppermute | solution.py:40
  8.2 0.0 copy-done.2
  8.3 5.0 %collective-permute-start.2 = (bf16[2,4,64,384]{3,2,1,0:T(8,128)(2,1)S(1)}, bf16[2,4,64,384]{3,2,1,0:T(8,128)(2,1)S(1)}, u32[]{:S(2)}, u32[]{:S(2)}) collective-permute-start(bf16[2,4,64,384]{3,2,1,0:T(8,128)(2,1)S(1)} %slice.8), channel_id=1, source_target_pairs={{0,48},{1,49},{2,50},{3,51},{4,52},{5,53},{6,54},{7,55},{8,56},{9,... | collective-permute-start | bytes 1179656 | tf_op jit(solution)/shard_map/ppermute | solution.py:40
  13.2 0.0 copy-start.1
  13.3 3.3 %copy-done.1 = bf16[3,3,3,384,384]{4,3,2,1,0:T(8,128)(2,1)S(1)} copy-done((bf16[3,3,3,384,384]{4,3,2,1,0:T(8,128)(2,1)S(1)}, bf16[3,3,3,384,384]{4,3,2,1,0:T(8,128)(2,1)}, u32[]{:S(2)}) %copy-start.1) | copy-done | bytes 7962648
  16.5 6.0 %shard_map.46 = (f32[2,448,384]{2,1,0:T(8,128)S(1)}, bf16[3,3456,384]{2,1,0:T(8,128)(2,1)S(1)}) custom-call(bf16[2,4,104,384]{3,2,1,0:T(8,128)(2,1)S(1)} %maximum_select_fusion.1.cells, f32[1,384]{1,0:T(1,128)S(1)} %reshape.13.gain, bf16[3,3456,384]{2,1,0:T(8,128)(2,1)S(1)} %bitcast.5), custom_call_target="tpu_custom_call" | custom-call | flops 5000000000 | bytes 1048576 | tf_op jit(solution)/shard_map/pallas_call | solution.py:184
  22.5 9.4 %collective-permute-done.2 = bf16[2,4,64,384]{3,2,1,0:T(8,128)(2,1)S(1)} collective-permute-done((bf16[2,4,64,384]{3,2,1,0:T(8,128)(2,1)S(1)}, bf16[2,4,64,384]{3,2,1,0:T(8,128)(2,1)S(1)}, u32[]{:S(2)}, u32[]{:S(2)}) %collective-permute-start.2) | collective-permute-done | bytes 393248 | tf_op jit(solution)/shard_map/ppermute | solution.py:40
  32.0 4.3 %collective-permute-start.5 = (bf16[2,4,64,384]{3,2,1,0:T(8,128)(2,1)S(1)}, bf16[2,4,64,384]{3,2,1,0:T(8,128)(2,1)S(1)}, u32[]{:S(2)}, u32[]{:S(2)}) collective-permute-start(bf16[2,4,64,384]{3,2,1,0:T(8,128)(2,1)S(1)} %collective-permute-done.2), channel_id=1, source_target_pairs={{48,32},{49,33},{50,34},{51,35},{52,36},{53,37},{54,38},{55,39},{5... | collective-permute-start | bytes 1179656 | tf_op jit(solution)/shard_map/ppermute | solution.py:40
  36.3 0.0 collective-permute-done.1.cells
  36.3 5.4 %collective-permute-start.6 = (bf16[2,4,40,384]{3,2,1,0:T(8,128)(2,1)S(1)}, bf16[2,4,40,384]{3,2,1,0:T(8,128)(2,1)S(1)}, u32[]{:S(2)}, u32[]{:S(2)}) collective-permute-start(bf16[2,4,40,384]{3,2,1,0:T(8,128)(2,1)S(1)} %slice.7), channel_id=1, source_target_pairs={{0,16},{1,17},{2,18},{3,19},{4,20},{5,21},{6,22},{7,23},{8,24},{9,... | collective-permute-start | bytes 737288 | tf_op jit(solution)/shard_map/ppermute | solution.py:40
  41.7 0.1 fusion
  41.8 1.2 %collective-permute-start.4 = (bf16[4,1,104,384]{3,2,1,0:T(8,128)(2,1)S(1)}, bf16[4,1,104,384]{3,2,1,0:T(8,128)(2,1)S(1)}, u32[]{:S(2)}, u32[]{:S(2)}) collective-permute-start(bf16[4,1,104,384]{3,2,1,0:T(8,128)(2,1)S(1)} %get-tuple-element.31), channel_id=1, source_target_pairs={{0,8},{1,9},{2,10},{3,11},{4,12},{5,13},{6,14},{7,15},{8,0},{9,1},... | collective-permute-start | bytes 958472 | tf_op jit(solution)/shard_map/ppermute | solution.py:40
  43.0 6.1 %collective-permute-start.3 = (bf16[4,1,104,384]{3,2,1,0:T(8,128)(2,1)S(1)}, bf16[4,1,104,384]{3,2,1,0:T(8,128)(2,1)S(1)}, u32[]{:S(2)}, u32[]{:S(2)}) collective-permute-start(bf16[4,1,104,384]{3,2,1,0:T(8,128)(2,1)S(1)} %get-tuple-element.32), channel_id=1, source_target_pairs={{1,8},{2,9},{3,10},{4,11},{5,12},{6,13},{7,14},{8,1},{9,2},{10,3},... | collective-permute-start | bytes 958472 | tf_op jit(solution)/shard_map/ppermute | solution.py:40
  49.1 9.5 %shard_map.47 = (f32[2,448,384]{2,1,0:T(8,128)S(1)}, f32[2,448,384]{2,1,0:T(8,128)S(1)}) custom-call(bf16[2,4,104,384]{3,2,1,0:T(8,128)(2,1)S(1)} %collective-permute-done.1.cells, f32[1,384]{1,0:T(1,128)S(1)} %reshape.13.gain, bf16[3,3456,384]{2,1,0:T(8,128)(2,1)S(1)} %get-tuple-element.22.weight, f32[2,448,384]{2,1,0:T(8,128)S(1)} %get-tuple-element.23.own), custom_call_target="tpu_custom_call" | custom-call | flops 10000000000 | bytes 1048576 | tf_op jit(solution)/shard_map/pallas_call | solution.py:184
  58.6 0.0 collective-permute-done.5.away
  58.6 0.0 collective-permute-done.6.near
  58.7 3.6 %collective-permute-start.7 = (bf16[2,1,104,384]{3,2,1,0:T(8,128)(2,1)S(1)}, bf16[2,1,104,384]{3,2,1,0:T(8,128)(2,1)S(1)}, u32[]{:S(2)}, u32[]{:S(2)}) collective-permute-start(bf16[2,1,104,384]{3,2,1,0:T(8,128)(2,1)S(1)} %pad_maximum_fusion), channel_id=1, source_target_pairs={{1,8},{2,9},{3,10},{4,11},{5,12},{6,13},{7,14},{8,1},{9,2},{10,3},... | collective-permute-start | bytes 479240 | tf_op jit(solution)/shard_map/ppermute | solution.py:40
  62.3 0.0 copy-start
  62.4 0.3 collective-permute-start.8
  62.6 5.4 %shard_map.48.middle = f32[2,448,384]{2,1,0:T(8,128)S(1)} custom-call(bf16[2,4,64,384]{3,2,1,0:T(8,128)(2,1)S(1)} %collective-permute-done.5.away, bf16[2,4,40,384]{3,2,1,0:T(8,128)(2,1)S(1)} %collective-permute-done.6.near, f32[1,384]{1,0:T(1,128)S(1)} %reshape.13.gain, bf16[3,3456,384]{2,1,0:T(8,128)(2,1)S(1)} %get-tuple-element.22.weight, ...), custom_call_target="tpu_custom_call" | custom-call | flops 5000000000 | bytes 1048576 | tf_op jit(solution)/shard_map/pallas_call | solution.py:184
  68.0 0.0 collective-permute-done.4.inner
  68.0 0.0 collective-permute-done.3.outer
  68.0 0.0 collective-permute-done.7.outer_old
  68.0 0.0 collective-permute-done.8.inner_old
  68.1 0.0 copy-done
  68.1 5.8 %shard_map.49 = (bf16[2,4,104,384]{3,2,1,0:T(8,128)(2,1)S(1)}, bf16[2,448,1152]{2,1,0:T(8,128)(2,1)S(1)}) custom-call(s32[1]{0:T(128)} %bitcast.core, bf16[4,1,104,384]{3,2,1,0:T(8,128)(2,1)S(1)} %collective-permute-done.3.outer, bf16[4,1,104,384]{3,2,1,0:T(8,128)(2,1)S(1)} %collective-permute-done.4.inner, ...), custom_call_target="tpu_custom_call" | custom-call | flops 5000000000 | bytes 1048576 | tf_op jit(solution)/shard_map/pallas_call | solution.py:184
  73.9 0.6 collective-permute-start.9
  74.5 1.1 %shard_map.50 = bf16[2,4,104,384]{3,2,1,0:T(8,128)(2,1)S(1)} custom-call(s32[1]{0:T(128)} %bitcast.core, bf16[2,448,1152]{2,1,0:T(8,128)(2,1)S(1)} %get-tuple-element.29.lines, bf16[1152,768]{1,0:T(8,128)(2,1)S(1)} %bitcast.4), custom_call_target="tpu_custom_call" | custom-call | flops 1000000000 | bytes 1048576 | tf_op jit(solution)/shard_map/pallas_call | solution.py:184
  75.5 0.6 collective-permute-done.9
  76.2 1.3 %maximum_select_fusion = bf16[2,8,104,384]{3,2,1,0:T(8,128)(2,1)} fusion(bf16[2,4,104,384]{3,2,1,0:T(8,128)(2,1)S(1)} %collective-permute-done.9, bf16[2,4,104,384]{3,2,1,0:T(8,128)(2,1)S(1)} %shard_map.50, pred[]{:T(512)S(6)} %eq.6), kind=kLoop, calls=%fused_computation.4 | loop fusion | flops 1916928 | bytes 2555905 | tf_op jit(solution)/shard_map/jit(_where)/select_n | solution.py:261
  (7 shorter events, 0.2 us)
Async XLA Ops:
  0.0 8.2 %copy-start.2 = (f32[384]{0:T(512)S(1)}, f32[384]{0:T(512)}, u32[]{:S(2)}) copy-start(f32[384]{0:T(512)} %param.5) | copy-start | bytes 4612
  1.1 2.0 %collective-permute-start = (bf16[1,4,104,384]{3,2,1,0:T(8,128)(2,1)S(1)}, bf16[1,4,104,384]{3,2,1,0:T(8,128)(2,1)S(1)}, u32[]{:S(2)}, u32[]{:S(2)}) collective-permute-start(bf16[1,4,104,384]{3,2,1,0:T(8,128)(2,1)S(1)} %get-tuple-element.34), channel_id=1, source_target_pairs={{0,8},{1,9},{2,10},{3,11},{4,12},{5,13},{6,14},{7,15},{8,0},{9,1},... | collective-permute-start | bytes 958472 | tf_op jit(solution)/shard_map/ppermute | solution.py:40
  3.3 33.0 %collective-permute-start.1 = (bf16[2,4,104,384]{3,2,1,0:T(8,128)(2,1)S(1)}, bf16[2,4,104,384]{3,2,1,0:T(8,128)(2,1)S(1)}, u32[]{:S(2)}, u32[]{:S(2)}) collective-permute-start(bf16[2,4,104,384]{3,2,1,0:T(8,128)(2,1)S(1)} %maximum_select_fusion.1.cells), channel_id=1, source_target_pairs={{0,16},{1,17},{2,18},{3,19},{4,20},{5,21},{6,22},{7,23},{8,24},{9,... | collective-permute-start | bytes 1916936 | tf_op jit(solution)/shard_map/ppermute | solution.py:40
  8.3 23.7 %collective-permute-start.2 = (bf16[2,4,64,384]{3,2,1,0:T(8,128)(2,1)S(1)}, bf16[2,4,64,384]{3,2,1,0:T(8,128)(2,1)S(1)}, u32[]{:S(2)}, u32[]{:S(2)}) collective-permute-start(bf16[2,4,64,384]{3,2,1,0:T(8,128)(2,1)S(1)} %slice.8), channel_id=1, source_target_pairs={{0,48},{1,49},{2,50},{3,51},{4,52},{5,53},{6,54},{7,55},{8,56},{9,... | collective-permute-start | bytes 1179656 | tf_op jit(solution)/shard_map/ppermute | solution.py:40
  13.2 3.3 %copy-start.1 = (bf16[3,3,3,384,384]{4,3,2,1,0:T(8,128)(2,1)S(1)}, bf16[3,3,3,384,384]{4,3,2,1,0:T(8,128)(2,1)}, u32[]{:S(2)}) copy-start(bf16[3,3,3,384,384]{4,3,2,1,0:T(8,128)(2,1)} %param.6) | copy-start | bytes 23887876
  32.0 26.6 %collective-permute-start.5 = (bf16[2,4,64,384]{3,2,1,0:T(8,128)(2,1)S(1)}, bf16[2,4,64,384]{3,2,1,0:T(8,128)(2,1)S(1)}, u32[]{:S(2)}, u32[]{:S(2)}) collective-permute-start(bf16[2,4,64,384]{3,2,1,0:T(8,128)(2,1)S(1)} %collective-permute-done.2), channel_id=1, source_target_pairs={{48,32},{49,33},{50,34},{51,35},{52,36},{53,37},{54,38},{55,39},{5... | collective-permute-start | bytes 1179656 | tf_op jit(solution)/shard_map/ppermute | solution.py:40
  36.3 22.3 %collective-permute-start.6 = (bf16[2,4,40,384]{3,2,1,0:T(8,128)(2,1)S(1)}, bf16[2,4,40,384]{3,2,1,0:T(8,128)(2,1)S(1)}, u32[]{:S(2)}, u32[]{:S(2)}) collective-permute-start(bf16[2,4,40,384]{3,2,1,0:T(8,128)(2,1)S(1)} %slice.7), channel_id=1, source_target_pairs={{0,16},{1,17},{2,18},{3,19},{4,20},{5,21},{6,22},{7,23},{8,24},{9,... | collective-permute-start | bytes 737288 | tf_op jit(solution)/shard_map/ppermute | solution.py:40
  41.8 26.2 %collective-permute-start.4 = (bf16[4,1,104,384]{3,2,1,0:T(8,128)(2,1)S(1)}, bf16[4,1,104,384]{3,2,1,0:T(8,128)(2,1)S(1)}, u32[]{:S(2)}, u32[]{:S(2)}) collective-permute-start(bf16[4,1,104,384]{3,2,1,0:T(8,128)(2,1)S(1)} %get-tuple-element.31), channel_id=1, source_target_pairs={{0,8},{1,9},{2,10},{3,11},{4,12},{5,13},{6,14},{7,15},{8,0},{9,1},... | collective-permute-start | bytes 958472 | tf_op jit(solution)/shard_map/ppermute | solution.py:40
  43.0 25.1 %collective-permute-start.3 = (bf16[4,1,104,384]{3,2,1,0:T(8,128)(2,1)S(1)}, bf16[4,1,104,384]{3,2,1,0:T(8,128)(2,1)S(1)}, u32[]{:S(2)}, u32[]{:S(2)}) collective-permute-start(bf16[4,1,104,384]{3,2,1,0:T(8,128)(2,1)S(1)} %get-tuple-element.32), channel_id=1, source_target_pairs={{1,8},{2,9},{3,10},{4,11},{5,12},{6,13},{7,14},{8,1},{9,2},{10,3},... | collective-permute-start | bytes 958472 | tf_op jit(solution)/shard_map/ppermute | solution.py:40
  58.7 9.3 %collective-permute-start.7 = (bf16[2,1,104,384]{3,2,1,0:T(8,128)(2,1)S(1)}, bf16[2,1,104,384]{3,2,1,0:T(8,128)(2,1)S(1)}, u32[]{:S(2)}, u32[]{:S(2)}) collective-permute-start(bf16[2,1,104,384]{3,2,1,0:T(8,128)(2,1)S(1)} %pad_maximum_fusion), channel_id=1, source_target_pairs={{1,8},{2,9},{3,10},{4,11},{5,12},{6,13},{7,14},{8,1},{9,2},{10,3},... | collective-permute-start | bytes 479240 | tf_op jit(solution)/shard_map/ppermute | solution.py:40
  62.3 5.7 %copy-start = (bf16[3,384,768]{2,1,0:T(8,128)(2,1)S(1)}, bf16[3,384,768]{2,1,0:T(8,128)(2,1)}, u32[]{:S(2)}) copy-start(bf16[3,384,768]{2,1,0:T(8,128)(2,1)} %param.7) | copy-start | bytes 5308420
  62.4 5.7 %collective-permute-start.8 = (bf16[2,1,104,384]{3,2,1,0:T(8,128)(2,1)S(1)}, bf16[2,1,104,384]{3,2,1,0:T(8,128)(2,1)S(1)}, u32[]{:S(2)}, u32[]{:S(2)}) collective-permute-start(bf16[2,1,104,384]{3,2,1,0:T(8,128)(2,1)S(1)} %pad_maximum_fusion.1), channel_id=1, source_target_pairs={{0,8},{1,9},{2,10},{3,11},{4,12},{5,13},{6,14},{7,15},{8,0},{9,1},... | collective-permute-start | bytes 479240 | tf_op jit(solution)/shard_map/ppermute | solution.py:40
  73.9 2.3 %collective-permute-start.9 = (bf16[2,4,104,384]{3,2,1,0:T(8,128)(2,1)S(1)}, bf16[2,4,104,384]{3,2,1,0:T(8,128)(2,1)S(1)}, u32[]{:S(2)}, u32[]{:S(2)}) collective-permute-start(bf16[2,4,104,384]{3,2,1,0:T(8,128)(2,1)S(1)} %get-tuple-element.30), channel_id=1, source_target_pairs={{0,8},{1,9},{2,10},{3,11},{4,12},{5,13},{6,14},{7,15},{8,0},{9,1},... | collective-permute-start | bytes 1916936 | tf_op jit(solution)/shard_map/ppermute | solution.py:40
